TPU v7x, 768 devices: a whole 4x8x12 slice. The times are simulated.
768 devices in a mesh: dp: 12 (over z), brick: 64 (over x, y, core).
Axes of the slice: x: 4, y: 8, z: 12, core: 2. Of those that a mesh axis runs over, the one named last changes fastest.
Arguments:
- records: bfloat16 [768, 64, 2, 6144], P(('dp', 'brick')), may hold values from -6 to 6
- positions: int32 [768, 64, 2], P(('dp', 'brick')), may hold values from -1 to 127, as said below
- weight: bfloat16 [2592, 192], P('dp'), may hold values from -0.125 to 0.125
- cotangent: bfloat16 [12, 256, 16, 3072], P('dp', 'brick'), may hold values from -0.0234375 to 0.0234375
Outputs:
- activation: bfloat16 [12, 256, 16, 3072], P('dp', 'brick')
- weight_grad: float32 [2592, 192], P('dp')
Inputs may be any that keep to these rules, and one draw needn't show every extreme that they name: Entry [d * 64 + s, o, r] is the brick position in owner o's slab of scene d of the r-th record that source s sends to o, or -1 for an empty slot. The live positions at one owner of one scene are distinct; in every scene some owner has all 128 of its slots filled.
All inputs are finite; a program needn't handle non-finite values.
Results may differ from a plain program's by a relative error of at most 0.0029.
Values may be sent and summed in bfloat16 or wider, within the bound.
No kernel may reach another device: no remote copies, remote signals or barrier semaphores. Data moves between devices by JAX's collectives and lax.ppermute only.
A program may use at most 64 MiB of HBM per device.

v0:
```python
import jax
import jax.numpy as jnp
from jax import lax
from jax.sharding import PartitionSpec as P

C_IN = 96
BS = 4
BX = 2
BY = 8
BZ = 8


def from_behind(block, axis, distance):
    devices = range(lax.axis_size(axis))
    route = [(i - distance, i) for i in devices if i - distance in devices]
    return lax.ppermute(block, axis, route)


def place_records(arrived, places, brick_x, brick_y, brick_z, side, channels):
    count = brick_x * brick_y * brick_z
    target = jnp.where(places >= 0, places, count)
    filled = jnp.zeros((count + 1, arrived.shape[1]), arrived.dtype).at[target].set(arrived)[:count]
    cubes = filled.reshape(brick_x, brick_y, brick_z, side, side, side, channels)
    cubes = cubes.transpose(0, 3, 1, 4, 2, 5, 6)
    return cubes.reshape(brick_x * side, brick_y * side, brick_z * side, channels)


def parity_split(voxels, boundary):
    padded = jnp.concatenate([boundary, voxels], axis=0)
    padded = jnp.pad(padded, ((0, 1), (1, 1), (1, 1), (0, 0)))
    half_x = padded.shape[0] // 2
    half_y = padded.shape[1] // 2
    half_z = padded.shape[2] // 2
    channels = padded.shape[3]
    split = padded.reshape(half_x, 2, half_y, 2, half_z, 2, channels)
    return split.transpose(1, 3, 5, 0, 2, 4, 6)


def column_block(classes, out_x, out_y, out_z):
    channels = classes.shape[-1]
    taps = []
    for offset_x in range(3):
        for offset_y in range(3):
            for offset_z in range(3):
                picked = classes[
                    offset_x % 2,
                    offset_y % 2,
                    offset_z % 2,
                    offset_x // 2 : offset_x // 2 + out_x,
                    offset_y // 2 : offset_y // 2 + out_y,
                    offset_z // 2 : offset_z // 2 + out_z,
                ]
                taps.append(picked.reshape(out_x * out_y * out_z, channels))
    return jnp.concatenate(taps, axis=1)


def body(records, positions, weight, cotangent):
    arrived, places = (
        lax.all_to_all(records, "brick", split_axis=1, concat_axis=0, tiled=True),
        lax.all_to_all(
            positions.astype(jnp.bfloat16), "brick", split_axis=1, concat_axis=0, tiled=True
        ),
    )
    arrived = arrived.reshape(-1, arrived.shape[-1])
    places = places.reshape(-1).astype(jnp.int32)
    voxels = place_records(arrived, places, BX, BY, BZ, BS, C_IN)
    boundary = from_behind(voxels[voxels.shape[0] - 1 :], "brick", 1)
    out_x = voxels.shape[0] // 2
    out_y = voxels.shape[1] // 2
    out_z = voxels.shape[2] // 2
    columns = column_block(parity_split(voxels, boundary), out_x, out_y, out_z)
    full_weight = lax.all_gather(weight, "dp", axis=0, tiled=True)
    linear = jnp.dot(columns, full_weight, preferred_element_type=jnp.float32)
    activation = jax.nn.silu(linear).astype(jnp.bfloat16)
    sigma = jax.nn.sigmoid(linear)
    slope = sigma * (1.0 + linear * (1.0 - sigma))
    upstream = cotangent.reshape(linear.shape[0], weight.shape[1])
    slope_grad = (upstream.astype(jnp.float32) * slope).astype(jnp.bfloat16)
    partial_grad = lax.dot_general(
        columns, slope_grad, (((0,), (0,)), ((), ())), preferred_element_type=jnp.float32
    )
    summed = lax.psum(partial_grad, "brick")
    weight_grad = lax.psum_scatter(summed, "dp", scatter_dimension=0, tiled=True)
    return (activation.reshape(cotangent.shape), weight_grad)


def solution(mesh):
    placed = (
        P(("dp", "brick"), None, None, None),
        P(("dp", "brick"), None, None),
        P("dp", None),
        P("dp", "brick", None, None),
    )
    return jax.shard_map(
        body,
        mesh=mesh,
        in_specs=placed,
        out_specs=(P("dp", "brick", None, None), P("dp", None)),
        check_vma=False,
    )
```

profile of v0, /device:TPU:1, one launch (start us, length us, event | category | flops | bytes accessed | tf_op | source)
XLA Modules:
  0.0 425.8 jit_solution(17270965308663684292)
XLA Ops:
  7.2 0.7 convert_element_type.30
  7.8 0.1 copy.18
  8.0 23.1 %all_to_all.8 = bf16[1,64,2]{2,0,1:T(2,128)(2,1)S(1)} all-to-all(bf16[1,64,2]{2,0,1:T(2,128)(2,1)S(1)} %copy.18), channel_id=1, replica_groups=mesh['dp'=12,'brick'=64] {'brick'}, dimensions={1} | all-to-all | bytes 512 | tf_op jit(solution)/shard_map/all_to_all | solution.py:60
  31.1 4.8 %all-to-all-start.1 = ((bf16[1,64,2,6144]{3,2,0,1:T(2,128)(2,1)}), bf16[1,64,2,6144]{3,2,0,1:T(2,128)(2,1)S(1)}, u32[]{:S(2)}, u32[]{:S(2)}) async-start(bf16[1,64,2,6144]{3,2,0,1:T(2,128)(2,1)} %bitcast.50), calls=%async_computation.1 | async-start | bytes 3145728 | tf_op jit(solution)/shard_map/all_to_all | solution.py:59
  35.9 0.0 reduce-scatter.4.cloned.1.call-start
  35.9 0.1 convert_reduce_fusion
  36.1 0.1 reshape.63
  36.2 39.5 %all-to-all-done.1 = bf16[1,64,2,6144]{3,2,0,1:T(2,128)(2,1)S(1)} async-done(((bf16[1,64,2,6144]{3,2,0,1:T(2,128)(2,1)}), bf16[1,64,2,6144]{3,2,0,1:T(2,128)(2,1)S(1)}, u32[]{:S(2)}, u32[]{:S(2)}) %all-to-all-start.1) | async-done | bytes 1572896 | tf_op jit(solution)/shard_map/all_to_all | solution.py:59
  75.7 0.6 reshape.69
  76.4 3.2 scatter_custom_fusion
  79.5 1.3 slice.116
  80.8 4.3 %reshape.59 = bf16[2,8,8,4,4,4,96]{6,5,4,3,2,1,0:T(4,128)(2,1)S(1)} reshape(bf16[128,6144]{1,0:T(8,128)(2,1)} %slice.116) | data formatting | bytes 3145728 | tf_op jit(solution)/shard_map/reshape | solution.py:23
  85.1 0.0 copy-start.5
  85.1 1.1 copy.20
  86.3 0.0 copy-start
  86.3 0.0 copy-start.4
  86.3 1.3 copy-done
  87.7 2.9 collective-permute-start
  90.6 0.0 copy-done.5
  90.6 32.0 %all-gather = bf16[12,216,192]{1,2,0:T(8,128)(2,1)S(1)} all-gather(bf16[1,216,192]{1,2,0:T(8,128)(2,1)S(1)} %bitcast.79), channel_id=1, replica_groups=mesh['dp'=12,'brick'=64] {'dp'}, dimensions={0}, use_global_device_ids=true | all-gather | bytes 1078272 | tf_op jit(solution)/shard_map/all_gather | solution.py:72
  122.6 1.5 copy.22
  124.1 0.0 copy-done.4
  124.1 0.5 reshape.64
  124.6 1.2 copy.24
  125.8 0.0 collective-permute-done
  125.8 3.4 fusion.8
  129.2 3.2 reshape.61
  132.4 2.4 copy.28
  134.7 1.9 fusion.17
  136.7 1.4 fusion.18
  138.0 0.0 copy-start.2
  138.0 10.2 %concatenate.7 = bf16[1024,2592]{1,0:T(8,128)(2,1)} concatenate(bf16[1024,96]{1,0:T(8,128)(2,1)} %bitcast.78, bf16[1024,96]{1,0:T(8,128)(2,1)} %bitcast.77, bf16[1024,96]{1,0:T(8,128)(2,1)} %bitcast.76, bf16[1024,96]{1,0:T(8,128)(2,1)} %bitcast.75, bf16[1024,96]{1,0:T(8,128)(2,1)} %bitcast.74, bf16[1024,96]{1,0:T(8,128)(2,1)} %bitcast.73, bf16[1024,96]{1,0:T(8,128)(2,1)} %bitcast.72, ...), dimensions={1} | concatenate | bytes 10616832 | tf_op jit(solution)/shard_map/concatenate | solution.py:54
  148.2 0.0 copy-done.2
  148.2 0.0 copy-start.1
  148.2 0.0 copy-start.3
  148.2 4.8 %multiply_convert_fusion.1 = (bf16[1024,192]{0,1:T(8,128)(2,1)S(1)}, f32[1024,192]{0,1:T(8,128)S(1)}) fusion(bf16[1024,2592]{1,0:T(8,128)(2,1)} %concatenate.7, bf16[2592,192]{1,0:T(8,128)(2,1)S(1)} %bitcast.51), kind=kOutput, calls=%fused_computation.21 | convolution fusion | flops 1020198912 | bytes 7483392 | tf_op jit(solution)/shard_map/dot_general | solution.py:73
  153.0 0.0 copy-done.1
  153.1 0.0 copy-done.3
  153.1 3.9 fusion.13
  156.9 0.0 reduce-scatter.4.cloned.1.call-update
  157.0 0.0 all-reduce.3.cloned.1.call-start
  157.0 52.2 %reduce-scatter.4.cloned.1.call-done = f32[216,192]{1,0:T(8,128)} async-done(((f32[2592,192]{1,0:T(8,128)}), f32[216,192]{1,0:T(8,128)}) %reduce-scatter.4.cloned.1.call-update) | async-done | bytes 165904
  209.2 1.7 copy.26
  210.9 0.0 all-reduce.3.cloned.1.call-update
  211.0 0.2 copy.23
  211.2 1.3 reshape.62
  212.5 204.8 %all-reduce.3.cloned.1.call-done = f32[216,192]{0,1:T(8,128)} async-done(((f32[216,192]{0,1:T(8,128)}), f32[216,192]{0,1:T(8,128)}) %all-reduce.3.cloned.1.call-update) | async-done | bytes 165904 | tf_op jit(solution)/shard_map/psum | solution.py:82
  417.3 1.6 copy.30
  (2 shorter events, 0.0 us)
Async XLA Ops:
  31.1 44.6 %all-to-all-start.1 = ((bf16[1,64,2,6144]{3,2,0,1:T(2,128)(2,1)}), bf16[1,64,2,6144]{3,2,0,1:T(2,128)(2,1)S(1)}, u32[]{:S(2)}, u32[]{:S(2)}) async-start(bf16[1,64,2,6144]{3,2,0,1:T(2,128)(2,1)} %bitcast.50), calls=%async_computation.1 | async-start | bytes 3145728 | tf_op jit(solution)/shard_map/all_to_all | solution.py:59
  35.9 173.3 %reduce-scatter.4.cloned.1.call-start = ((), (), s32[]{:S(2)}) async-start(), calls=%async_computation.4 | async-start | bytes 2875392
  85.1 5.5 %copy-start.5 = (bf16[216,192]{0,1:T(8,128)(2,1)S(1)}, bf16[216,192]{0,1:T(8,128)(2,1)}, u32[]{:S(2)}) copy-start(bf16[216,192]{0,1:T(8,128)(2,1)} %param.6) | copy-start | bytes 248836
  86.3 1.4 copy-start
  86.3 37.8 %copy-start.4 = (bf16[1,4,16,3072]{3,2,1,0:T(8,128)(2,1)S(1)}, bf16[1,4,16,3072]{3,2,1,0:T(8,128)(2,1)}, u32[]{:S(2)}) copy-start(bf16[1,4,16,3072]{3,2,1,0:T(8,128)(2,1)} %param.7) | copy-start | bytes 1179652
  87.7 38.1 %collective-permute-start = (bf16[1,32,32,96]{3,2,1,0:T(8,128)(2,1)S(1)}, bf16[1,32,32,96]{3,2,1,0:T(8,128)(2,1)}, u32[]{:S(2)}, u32[]{:S(2)}) collective-permute-start(bf16[1,32,32,96]{3,2,1,0:T(8,128)(2,1)S(1)} %slice.117), channel_id=1, source_target_pairs={{0,1},{1,2},{2,3},{3,4},{4,5},{5,6},{6,7},{7,8},{8,9},{9,10},{10,1... | collective-permute-start | bytes 589832 | tf_op jit(solution)/shard_map/ppermute | solution.py:16
  138.0 10.2 %copy-start.2 = (bf16[12,216,192]{2,1,0:T(8,128)(2,1)S(1)}, bf16[12,216,192]{2,1,0:T(8,128)(2,1)}, u32[]{:S(2)}) copy-start(bf16[12,216,192]{2,1,0:T(8,128)(2,1)} %copy.22) | copy-start | bytes 2985988
  148.2 4.8 %copy-start.1 = (bf16[1024,2592]{1,0:T(8,128)(2,1)S(1)}, bf16[1024,2592]{1,0:T(8,128)(2,1)}, u32[]{:S(2)}) copy-start(bf16[1024,2592]{1,0:T(8,128)(2,1)} %concatenate.7) | copy-start | bytes 15925252
  148.2 4.8 %copy-start.3 = (f32[1024,192]{0,1:T(8,128)S(1)}, f32[1024,192]{0,1:T(8,128)}, u32[]{:S(2)}) copy-start(f32[1024,192]{0,1:T(8,128)} %copy.24) | copy-start | bytes 2359300
  157.0 260.3 %all-reduce.3.cloned.1.call-start = ((), (), s32[]{:S(2)}) async-start(), calls=%async_computation.3 | async-start | bytes 393216 | tf_op jit(solution)/shard_map/psum | solution.py:82
Sparse Core Ops, SparseCore 0:
  157.1 52.0 reduce-scatter.3
  213.2 204.0 all-reduce.2
where the time goes:
time: 428 us; the launch traced here: 426 us
  waiting for transfers between devices  297 us (69%)
  blocking collectives  55.1 us (13%)
  local copies, waits for them, and re-layouts  39.2 us (9%)
  between operations  14.2 us (3%)
  matrix products  8.67 us (2%)
  starting transfers between devices  7.77 us (2%)
    psum x1, waiting for transfers between devices, body(): summed = lax.psum(partial_grad, 'brick')  205 us
    unnamed x3, waiting for transfers between devices  52.2 us
    all_to_all x1, waiting for transfers between devices, body(): lax.all_to_all(records, 'brick', split_axis=1, concat_axis=0, tiled=True)  39.5 us
    all_gather x1, blocking collectives, body(): full_weight = lax.all_gather(weight, 'dp', axis=0, tiled=True)  32 us
    all_to_all x1, blocking collectives, body(): lax.all_to_all(positions.astype(jnp.bfloat16), 'brick', split_axis=1, con...  23.1 us
    concatenate x1, local copies, waits for them, and re-layouts, column_block(): return jnp.concatenate(taps, axis=1)  10.2 us
  transfers between devices with their start and end apart: 4, of which 3 were waited for; matrix products, arithmetic and copies ran while one was open for 1% of the time, Pallas kernels for 0%

commit v1 on v0

v1 whole, which is shorter than its diff:
```python
import jax
import jax.numpy as jnp
from jax import lax
from jax.experimental import pallas as pl
from jax.experimental.pallas import tpu as pltpu
from jax.sharding import PartitionSpec as P

C_IN = 96
C_OUT = 192
REC = 6144
NPOS = 128
LINE = 384
DEPTH = 512
TAPS = 9
N_DP = 12
N_BRICK = 64
SHARD = 216
SPLIT = 112
PIECE = 6
ROWS = N_BRICK * PIECE
VMEM = pl.BlockSpec(memory_space=pltpu.VMEM)
F32 = jnp.float32
BF16 = jnp.bfloat16


def params():
    return pltpu.CompilerParams(vmem_limit_bytes=56 * 1024 * 1024)


def brick_rows(shape, dim):
    q = lax.broadcasted_iota(jnp.int32, shape, dim)
    return q >> 4, (q >> 3) & 1, q & 7


def rim_kernel(arrived_ref, rim_ref):
    places = arrived_ref[:, REC : REC + NPOS].astype(F32).T
    m = lax.broadcasted_iota(jnp.int32, (64, NPOS), 0)
    wanted = 64 + (m & 7) * 8 + (m >> 3)
    pick = jnp.where(places[:64] == wanted.astype(F32), 1.0, 0.0).astype(BF16)
    rim_ref[...] = jnp.dot(
        pick, arrived_ref[:, 12 * LINE : REC], preferred_element_type=F32
    ).astype(BF16)


def weight_kernel(weight_ref, wide_ref):
    wide_ref[...] = jnp.zeros_like(wide_ref)
    for tap in range(TAPS):
        block = weight_ref[tap * 288 : (tap + 1) * 288, :]
        wide_ref[tap * DEPTH + 32 : tap * DEPTH + 320, 0:C_OUT] = block
        wide_ref[tap * DEPTH + 224 : tap * DEPTH + 512, C_OUT : 2 * C_OUT] = block


def layer_kernel(
    arrived_ref, rim_ref, wide_ref, cotangent_ref, activation_ref, terms_ref,
    columns, linear, upstream, result, slopes, packed,
):
    places = arrived_ref[:, REC : REC + NPOS].astype(F32).T
    bz, bx, by = brick_rows((NPOS, NPOS), 0)
    rz, rx, ry = brick_rows((NPOS, 64), 0)
    m = lax.broadcasted_iota(jnp.int32, (NPOS, 64), 1)

    def picker(sx, sy, sz):
        inside = (bx >= sx) & (by >= sy) & (bz >= sz)
        wanted = jnp.where(inside, (bx - sx) * 64 + (by - sy) * 8 + bz - sz, -2)
        return jnp.where(places == wanted.astype(F32), 1.0, 0.0).astype(BF16)

    def rim_picker(sy, sz):
        inside = (rx == 0) & (ry >= sy) & (rz >= sz)
        wanted = jnp.where(inside, (rz - sz) * 8 + ry - sy, -2)
        return jnp.where(m == wanted, 1.0, 0.0).astype(BF16)

    for sx in range(2):
        for sy in range(2):
            pick = [picker(sx, sy, sz) for sz in range(2)]
            if sx:
                rim_pick = [rim_picker(sy, sz) for sz in range(2)]
            for vx in [3] if sx else range(4):
                for vy in [3] if sy else range(4):
                    at = (vx * 4 + vy) * LINE
                    line = jnp.dot(pick[0], arrived_ref[:, at : at + LINE], preferred_element_type=F32)
                    before = jnp.dot(
                        pick[1], arrived_ref[:, at + 256 : at + LINE], preferred_element_type=F32
                    )
                    if sx:
                        at = vy * LINE
                        line += jnp.dot(
                            rim_pick[0], rim_ref[:, at : at + LINE], preferred_element_type=F32
                        )
                        before += jnp.dot(
                            rim_pick[1], rim_ref[:, at + 256 : at + LINE], preferred_element_type=F32
                        )
                    line = line.astype(BF16)
                    before = before.astype(BF16)
                    ux = vx - 4 * sx
                    uy = vy - 4 * sy
                    for i in range(2):
                        for j in range(2):
                            a = ux + 1 - 2 * i
                            b = uy + 1 - 2 * j
                            if 0 <= a <= 2 and 0 <= b <= 2:
                                row = (i * 2 + j) * NPOS
                                col = (a * 3 + b) * DEPTH
                                columns[row : row + NPOS, col : col + 128] = before
                                columns[row : row + NPOS, col + 128 : col + DEPTH] = line

    linear[...] = jnp.dot(columns[...], wide_ref[...], preferred_element_type=F32)
    for tile in range(24):
        for x in range(4):
            upstream[x, tile] = cotangent_ref[x, :, tile * 128 : (tile + 1) * 128].astype(F32)
    for i in range(2):
        for j in range(2):
            for z in range(8):
                row = (i * 2 + j) * NPOS + z * 16
                value = linear[row : row + 16, :]
                sigma = 1.0 / (1.0 + jnp.exp(-value))
                active = value * sigma
                slope = sigma * (1.0 + value * (1.0 - sigma))
                incoming = []
                for tile in range(3):
                    lanes = slice(tile * 128, (tile + 1) * 128)
                    parts = []
                    for x in range(2):
                        at = (x * 2 + i, z * 3 + tile, pl.ds(j, 8, stride=2), slice(None))
                        parts.append(upstream[at])
                        result[at] = active[x * 8 : x * 8 + 8, lanes]
                    incoming.append(jnp.concatenate(parts, axis=0))
                incoming = jnp.concatenate(incoming, axis=1)
                slopes[row : row + 16, :] = (incoming * slope).astype(BF16)
    for tile in range(24):
        for x in range(4):
            activation_ref[x, :, tile * 128 : (tile + 1) * 128] = result[x, tile].astype(BF16)

    for d in range(N_DP):
        packed[d * ROWS + SHARD + SPLIT - 8 : (d + 1) * ROWS, :] = jnp.zeros(
            (ROWS - SHARD - SPLIT + 8, 128), F32
        )
    for tap in range(TAPS):
        product = lax.dot_general(
            columns[:, tap * DEPTH : (tap + 1) * DEPTH], slopes[...],
            (((0,), (0,)), ((), ())), preferred_element_type=F32,
        )
        block = product[32:320, 0:C_OUT] + product[224:512, C_OUT : 2 * C_OUT]
        start = tap * 288
        while start < (tap + 1) * 288:
            d, row = divmod(start, SHARD)
            stop = min((tap + 1) * 288, d * SHARD + (SPLIT if row < SPLIT else SHARD))
            part = block[start - tap * 288 : stop - tap * 288]
            size = stop - start
            to = d * ROWS + row
            packed[to : to + size, :] = part[:, 0:128]
            if row < SPLIT:
                packed[to + SHARD : to + SHARD + size, 0:64] = part[:, 128:C_OUT]
            else:
                to = to + SHARD - SPLIT
                packed[to : to + size, 64:128] = part[:, 128:C_OUT]
            start = stop
    for piece in range(N_BRICK):
        terms_ref[piece] = packed[pl.ds(piece, N_DP * PIECE, stride=N_BRICK), :].astype(BF16)


def brick_sum_kernel(terms_ref, sums_ref):
    total = terms_ref[0].astype(F32)
    for source in range(1, N_BRICK):
        total += terms_ref[source].astype(F32)
    for d in range(N_DP):
        sums_ref[d] = total[d * PIECE : (d + 1) * PIECE]


def scene_sum_kernel(sums_ref, copies_ref):
    total = sums_ref[0]
    for source in range(1, N_DP):
        total += sums_ref[source]
    for target in range(N_BRICK):
        copies_ref[target] = total


def unpack_kernel(pieces_ref, grad_ref, packed):
    for row in range(PIECE):
        packed[row * N_BRICK : (row + 1) * N_BRICK, :] = pieces_ref[:, row, :]
    grad_ref[:, 0:128] = packed[0:SHARD, :]
    grad_ref[0:SPLIT, 128:C_OUT] = packed[SHARD : SHARD + SPLIT, 0:64]
    grad_ref[SPLIT:SHARD, 128:C_OUT] = packed[SHARD : 2 * SHARD - SPLIT, 64:128]


def call(kernel, out, scratch=(), count=1):
    return pl.pallas_call(
        kernel,
        out_shape=out,
        in_specs=[VMEM] * count,
        out_specs=jax.tree.map(lambda _: VMEM, out),
        scratch_shapes=list(scratch),
        compiler_params=params(),
    )


def spread(block, axis):
    return lax.all_to_all(block, axis, split_axis=0, concat_axis=0, tiled=True)


def body(records, positions, weight, cotangent):
    shape = jax.ShapeDtypeStruct
    places = jnp.broadcast_to(positions.astype(BF16)[..., None], positions.shape + (NPOS,))
    sent = jnp.concatenate([records, places], axis=3).reshape(N_BRICK, 2, REC + NPOS)
    arrived = spread(sent, "brick").reshape(NPOS, REC + NPOS)
    full_weight = lax.all_gather(weight, "dp", axis=0, tiled=True)
    wide = call(weight_kernel, shape((TAPS * DEPTH, LINE), BF16))(full_weight)
    arrived, wide = lax.optimization_barrier((arrived, wide))
    rim = call(rim_kernel, shape((64, 4 * LINE), BF16))(arrived)
    rim = lax.ppermute(rim, "brick", [(i, i + 1) for i in range(N_BRICK - 1)])
    activation, terms = call(
        layer_kernel,
        (shape((4, 16, 8 * LINE), BF16), shape((N_BRICK, N_DP * PIECE, 128), BF16)),
        [
            pltpu.VMEM((4 * NPOS, TAPS * DEPTH), BF16),
            pltpu.VMEM((4 * NPOS, LINE), F32),
            pltpu.VMEM((4, 24, 16, 128), F32),
            pltpu.VMEM((4, 24, 16, 128), F32),
            pltpu.VMEM((4 * NPOS, LINE), BF16),
            pltpu.VMEM((N_DP * ROWS, 128), F32),
        ],
        4,
    )(arrived, rim, wide, cotangent.reshape(4, 16, 8 * LINE))
    sums = call(brick_sum_kernel, shape((N_DP, PIECE, 128), F32))(spread(terms, "brick"))
    copies = call(scene_sum_kernel, shape((N_BRICK, PIECE, 128), F32))(spread(sums, "dp"))
    grad = call(unpack_kernel, shape((SHARD, C_OUT), F32), [pltpu.VMEM((ROWS, 128), F32)])(
        spread(copies, "brick")
    )
    return activation.reshape(cotangent.shape), grad


def solution(mesh):
    placed = (
        P(("dp", "brick"), None, None, None),
        P(("dp", "brick"), None, None),
        P("dp", None),
        P("dp", "brick", None, None),
    )
    return jax.shard_map(
        body,
        mesh=mesh,
        in_specs=placed,
        out_specs=(P("dp", "brick", None, None), P("dp", None)),
        check_vma=False,
    )
```

time: 428 us -> 172 us (0.40)
  waiting for transfers between devices: 297 us -> 6.17 us
  blocking collectives: 55.1 us -> 111 us
  local copies, waits for them, and re-layouts: 39.2 us -> 5.68 us
  Pallas kernels: 0 us -> 22.8 us
  between operations: 14.2 us -> 0.67 us
  starting transfers between devices: 7.77 us -> 20.4 us
  matrix products: 8.67 us -> 0 us
    psum x1 -> x0, waiting for transfers between devices: 205 us -> none  [body(): summed = lax.psum(partial_grad, 'brick')]
    all_to_all x1 -> x3, blocking collectives: 23.1 us -> 78.8 us  [spread(): return lax.all_to_all(block, axis, split_axis=0, concat_axis=0, tiled=True)]
    unnamed x3 -> x0, waiting for transfers between devices: 52.2 us -> none
    all_to_all x1, waiting for transfers between devices: 39.5 us -> 3.27 us  [spread(): return lax.all_to_all(block, axis, split_axis=0, concat_axis=0, tiled=True)]
    pallas_call x0 -> x6, Pallas kernels: none -> 22.8 us  [the longest x1 11.4 us: body(): call(layer_kernel, (shape((4, 16, 8 * LINE), BF16), shape((N_BRICK, N_DP...]
    reshape x5 -> x1, local copies, waits for them, and re-layouts: 11.8 us -> 1.51 us  [body(): arrived = spread(sent, 'brick').reshape(NPOS, REC + NPOS)]
    concatenate x1 -> x0, local copies, waits for them, and re-layouts: 10.2 us -> none  [column_block(): return jnp.concatenate(taps, axis=1)]
    all_to_all x1, starting transfers between devices: 4.78 us -> 14.8 us  [spread(): return lax.all_to_all(block, axis, split_axis=0, concat_axis=0, tiled=True)]
  transfers between devices with their start and end apart: 4 -> 2, of which waited for: 3 -> 2; matrix products, arithmetic and copies ran while one was open for 1% -> 1% of each run, Pallas kernels for 0% -> 2%
where the time goes in v1:
time: 172 us; the launch traced here: 171 us
  blocking collectives  111 us (65%)
  Pallas kernels  22.8 us (13%)
  starting transfers between devices  20.4 us (12%)
  waiting for transfers between devices  6.17 us (4%)
  local copies, waits for them, and re-layouts  5.68 us (3%)
  other arithmetic  4.74 us (3%)
    all_to_all x3, blocking collectives, spread(): return lax.all_to_all(block, axis, split_axis=0, concat_axis=0, tiled=True)  78.8 us
    all_gather x1, blocking collectives, body(): full_weight = lax.all_gather(weight, 'dp', axis=0, tiled=True)  32 us
    all_to_all x1, starting transfers between devices, spread(): return lax.all_to_all(block, axis, split_axis=0, concat_axis=0, tiled=True)  14.8 us
    pallas_call x1, Pallas kernels, body(): call(layer_kernel, (shape((4, 16, 8 * LINE), BF16), shape((N_BRICK, N_DP...  11.4 us
    ppermute x1, starting transfers between devices, body(): rim = lax.ppermute(rim, 'brick', [(i, i + 1) for i in range(N_BRICK - 1)])  5.6 us
    reshape x1, other arithmetic, body(): jnp.concatenate([records, places], axis=3).reshape(N_BRICK, 2, REC + NPOS)  4.05 us
    pallas_call x1, Pallas kernels, body(): wide = call(weight_kernel, shape((TAPS * DEPTH, LINE), BF16))(full_weight)  3.75 us
  transfers between devices with their start and end apart: 2, of which 2 were waited for; matrix products, arithmetic and copies ran while one was open for 1% of the time, Pallas kernels for 2%

profile of v1, /device:TPU:1, one launch (start us, length us, event | category | flops | bytes accessed | tf_op | source)
XLA Modules:
  0.0 171.2 jit_solution(1771391803699675993)
XLA Ops:
  0.6 0.7 convert_bitcast_fusion
  1.3 0.1 copy.9
  1.4 0.1 broadcast_in_dim.9
  1.6 4.1 %maximum_bitcast_fusion = bf16[64,2,6272]{2,1,0:T(2,128)(2,1)} fusion(bf16[1,64,2,128]{3,2,1,0:T(2,128)(2,1)S(1)} %broadcast_in_dim.9, bf16[1,64,2,6144]{3,2,1,0:T(2,128)(2,1)} %param.4), kind=kLoop, calls=%fused_computation | loop fusion | flops 3211264 | bytes 3211264 | tf_op jit(solution)/shard_map/reshape | solution.py:203
  5.6 0.0 copy-start.1
  5.6 14.8 %all-to-all-start = ((bf16[64,2,6272]{2,1,0:T(2,128)(2,1)}), bf16[64,2,6272]{2,1,0:T(2,128)(2,1)S(1)}, u32[]{:S(2)}, u32[]{:S(2)}) async-start(bf16[64,2,6272]{2,1,0:T(2,128)(2,1)} %maximum_bitcast_fusion), calls=%async_computation | async-start | bytes 3211264 | tf_op jit(solution)/shard_map/all_to_all | solution.py:197
  20.4 0.0 copy-done.1
  20.4 32.0 %all-gather = bf16[12,216,192]{1,2,0:T(8,128)(2,1)S(1)} all-gather(bf16[1,216,192]{1,2,0:T(8,128)(2,1)S(1)} %bitcast.10), channel_id=1, replica_groups=mesh['dp'=12,'brick'=64] {'dp'}, dimensions={0}, use_global_device_ids=true | all-gather | bytes 1078272 | tf_op jit(solution)/shard_map/all_gather | solution.py:205
  52.4 1.5 copy.10
  53.9 3.8 %shard_map.59.wide_ref = bf16[4608,384]{1,0:T(8,128)(2,1)} custom-call(bf16[2592,192]{1,0:T(8,128)(2,1)} %bitcast.8), custom_call_target="tpu_custom_call" | custom-call | tf_op jit(solution)/shard_map/pallas_call | solution.py:206
  57.7 3.3 %all-to-all-done = bf16[64,2,6272]{2,1,0:T(2,128)(2,1)S(1)} async-done(((bf16[64,2,6272]{2,1,0:T(2,128)(2,1)}), bf16[64,2,6272]{2,1,0:T(2,128)(2,1)S(1)}, u32[]{:S(2)}, u32[]{:S(2)}) %all-to-all-start) | async-done | bytes 1605664 | tf_op jit(solution)/shard_map/all_to_all | solution.py:197
  60.9 1.5 reshape.20.arrived_ref
  62.4 2.3 %shard_map.60 = bf16[64,1536]{1,0:T(8,128)(2,1)} custom-call(bf16[128,6272]{1,0:T(8,128)(2,1)} %reshape.20.arrived_ref), custom_call_target="tpu_custom_call" | custom-call | tf_op jit(solution)/shard_map/pallas_call | solution.py:208
  64.8 5.6 %collective-permute-start = (bf16[64,1536]{1,0:T(8,128)(2,1)}, bf16[64,1536]{1,0:T(8,128)(2,1)S(1)}, u32[]{:S(2)}, u32[]{:S(2)}) collective-permute-start(bf16[64,1536]{1,0:T(8,128)(2,1)} %shard_map.60), channel_id=1, source_target_pairs={{0,1},{1,2},{2,3},{3,4},{4,5},{5,6},{6,7},{7,8},{8,9},{9,10},{10,1... | collective-permute-start | bytes 589832 | tf_op jit(solution)/shard_map/ppermute | solution.py:209
  70.4 2.9 %collective-permute-done.rim_ref = bf16[64,1536]{1,0:T(8,128)(2,1)S(1)} collective-permute-done((bf16[64,1536]{1,0:T(8,128)(2,1)}, bf16[64,1536]{1,0:T(8,128)(2,1)S(1)}, u32[]{:S(2)}, u32[]{:S(2)}) %collective-permute-start) | collective-permute-done | bytes 196640 | tf_op jit(solution)/shard_map/ppermute | solution.py:209
  73.3 0.0 copy-start
  73.3 0.7 copy-done
  74.0 11.4 %shard_map.61 = (bf16[4,16,3072]{2,1,0:T(8,128)(2,1)}, bf16[64,72,128]{2,1,0:T(8,128)(2,1)}) custom-call(bf16[128,6272]{1,0:T(8,128)(2,1)} %reshape.20.arrived_ref, bf16[64,1536]{1,0:T(8,128)(2,1)} %copy-done, bf16[4608,384]{1,0:T(8,128)(2,1)} %shard_map.59.wide_ref, bf16[4,16,3072]{2,1,0:T(8,128)(2,1)} %bitcast.9), custom_call_target="tpu_custom_call" | custom-call | tf_op jit(solution)/shard_map/pallas_call | solution.py:210
  85.4 43.7 %all_to_all.20.terms_ref = bf16[64,72,128]{2,1,0:T(8,128)(2,1)} all-to-all(bf16[64,72,128]{2,1,0:T(8,128)(2,1)} %get-tuple-element.9), channel_id=1, replica_groups=mesh['dp'=12,'brick'=64] {'brick'}, dimensions={0} | all-to-all | bytes 2359296 | tf_op jit(solution)/shard_map/all_to_all | solution.py:197
  129.1 2.1 %shard_map.62 = f32[12,6,128]{2,1,0:T(8,128)} custom-call(bf16[64,72,128]{2,1,0:T(8,128)(2,1)} %all_to_all.20.terms_ref), custom_call_target="tpu_custom_call" | custom-call | tf_op jit(solution)/shard_map/pallas_call | solution.py:223
  131.2 15.1 %all_to_all.21.sums_ref = f32[12,6,128]{2,1,0:T(8,128)} all-to-all(f32[12,6,128]{2,1,0:T(8,128)} %shard_map.62), channel_id=1, replica_groups=mesh['dp'=12,'brick'=64] {'dp'}, dimensions={0} | all-to-all | bytes 73728 | tf_op jit(solution)/shard_map/all_to_all | solution.py:197
  146.3 1.5 shard_map.63
  147.8 20.0 %all_to_all.22.pieces_ref = f32[64,6,128]{2,1,0:T(8,128)} all-to-all(f32[64,6,128]{2,1,0:T(8,128)} %shard_map.63), channel_id=1, replica_groups=mesh['dp'=12,'brick'=64] {'brick'}, dimensions={0} | all-to-all | bytes 393216 | tf_op jit(solution)/shard_map/all_to_all | solution.py:197
  167.8 1.7 %shard_map.64 = f32[216,192]{1,0:T(8,128)} custom-call(f32[64,6,128]{2,1,0:T(8,128)} %all_to_all.22.pieces_ref), custom_call_target="tpu_custom_call" | custom-call | tf_op jit(solution)/shard_map/pallas_call | solution.py:225
  169.5 1.7 %copy.11 = f32[216,192]{0,1:T(8,128)} copy(f32[216,192]{1,0:T(8,128)} %shard_map.64) | data formatting | bytes 331776
Async XLA Ops:
  5.6 14.8 %copy-start.1 = (bf16[216,192]{0,1:T(8,128)(2,1)S(1)}, bf16[216,192]{0,1:T(8,128)(2,1)}, u32[]{:S(2)}) copy-start(bf16[216,192]{0,1:T(8,128)(2,1)} %param.6) | copy-start | bytes 248836
  5.6 55.3 %all-to-all-start = ((bf16[64,2,6272]{2,1,0:T(2,128)(2,1)}), bf16[64,2,6272]{2,1,0:T(2,128)(2,1)S(1)}, u32[]{:S(2)}, u32[]{:S(2)}) async-start(bf16[64,2,6272]{2,1,0:T(2,128)(2,1)} %maximum_bitcast_fusion), calls=%async_computation | async-start | bytes 3211264 | tf_op jit(solution)/shard_map/all_to_all | solution.py:197
  64.8 8.5 %collective-permute-start = (bf16[64,1536]{1,0:T(8,128)(2,1)}, bf16[64,1536]{1,0:T(8,128)(2,1)S(1)}, u32[]{:S(2)}, u32[]{:S(2)}) collective-permute-start(bf16[64,1536]{1,0:T(8,128)(2,1)} %shard_map.60), channel_id=1, source_target_pairs={{0,1},{1,2},{2,3},{3,4},{4,5},{5,6},{6,7},{7,8},{8,9},{9,10},{10,1... | collective-permute-start | bytes 589832 | tf_op jit(solution)/shard_map/ppermute | solution.py:209
  73.3 0.7 copy-start

commit v2 on v1

--- a/solution.py
+++ b/solution.py
@@ -14,17 +14,34 @@
 TAPS = 9
 N_DP = 12
 N_BRICK = 64
+N_CHIP = 32
 SHARD = 216
 SPLIT = 112
 PIECE = 6
 ROWS = N_BRICK * PIECE
+BRICK = ("x", "y", "core")
+ANY = pl.BlockSpec(memory_space=pl.ANY)
 VMEM = pl.BlockSpec(memory_space=pltpu.VMEM)
 F32 = jnp.float32
 BF16 = jnp.bfloat16
 
 
-def params():
-    return pltpu.CompilerParams(vmem_limit_bytes=56 * 1024 * 1024)
+def join_kernel(records_ref, places_ref, sent_ref, sems):
+    copies = []
+    for part in range(8):
+        rows = pl.ds(part * 8, 8)
+        copies.append(
+            pltpu.make_async_copy(
+                records_ref.at[rows], sent_ref.at[rows, :, pl.ds(0, REC)], sems.at[part]
+            )
+        )
+    copies.append(
+        pltpu.make_async_copy(places_ref, sent_ref.at[:, :, pl.ds(REC, NPOS)], sems.at[8])
+    )
+    for copy in copies:
+        copy.start()
+    for copy in copies:
+        copy.wait()
 
 
 def brick_rows(shape, dim):
@@ -32,13 +49,13 @@
     return q >> 4, (q >> 3) & 1, q & 7
 
 
-def rim_kernel(arrived_ref, rim_ref):
-    places = arrived_ref[:, REC : REC + NPOS].astype(F32).T
+def rim_kernel(tail_ref, rim_ref):
+    places = tail_ref[:, 4 * LINE :].astype(F32).T
     m = lax.broadcasted_iota(jnp.int32, (64, NPOS), 0)
     wanted = 64 + (m & 7) * 8 + (m >> 3)
     pick = jnp.where(places[:64] == wanted.astype(F32), 1.0, 0.0).astype(BF16)
     rim_ref[...] = jnp.dot(
-        pick, arrived_ref[:, 12 * LINE : REC], preferred_element_type=F32
+        pick, tail_ref[:, 0 : 4 * LINE], preferred_element_type=F32
     ).astype(BF16)
 
 
@@ -51,7 +68,7 @@
 
 
 def layer_kernel(
-    arrived_ref, rim_ref, wide_ref, cotangent_ref, activation_ref, terms_ref,
+    core_ref, arrived_ref, rim_ref, wide_ref, cotangent_ref, activation_ref, kept_ref, given_ref,
     columns, linear, upstream, result, slopes, packed,
 ):
     places = arrived_ref[:, REC : REC + NPOS].astype(F32).T
@@ -154,13 +171,15 @@
                 to = to + SHARD - SPLIT
                 packed[to : to + size, 64:128] = part[:, 128:C_OUT]
             start = stop
-    for piece in range(N_BRICK):
-        terms_ref[piece] = packed[pl.ds(piece, N_DP * PIECE, stride=N_BRICK), :].astype(BF16)
-
-
-def brick_sum_kernel(terms_ref, sums_ref):
+    core = core_ref[0]
+    for chip in range(N_CHIP):
+        kept_ref[chip] = packed[pl.ds(2 * chip + core, N_DP * PIECE, stride=N_BRICK), :]
+        given_ref[chip] = packed[pl.ds(2 * chip + 1 - core, N_DP * PIECE, stride=N_BRICK), :]
+
+
+def chip_sum_kernel(terms_ref, sums_ref):
     total = terms_ref[0].astype(F32)
-    for source in range(1, N_BRICK):
+    for source in range(1, N_CHIP):
         total += terms_ref[source].astype(F32)
     for d in range(N_DP):
         sums_ref[d] = total[d * PIECE : (d + 1) * PIECE]
@@ -177,19 +196,19 @@
 def unpack_kernel(pieces_ref, grad_ref, packed):
     for row in range(PIECE):
         packed[row * N_BRICK : (row + 1) * N_BRICK, :] = pieces_ref[:, row, :]
-    grad_ref[:, 0:128] = packed[0:SHARD, :]
-    grad_ref[0:SPLIT, 128:C_OUT] = packed[SHARD : SHARD + SPLIT, 0:64]
-    grad_ref[SPLIT:SHARD, 128:C_OUT] = packed[SHARD : 2 * SHARD - SPLIT, 64:128]
-
-
-def call(kernel, out, scratch=(), count=1):
+    grad_ref[0:128, :] = packed[0:SHARD, :].T
+    grad_ref[128:C_OUT, 0:SPLIT] = packed[SHARD : SHARD + SPLIT, 0:64].T
+    grad_ref[128:C_OUT, SPLIT:SHARD] = packed[SHARD : 2 * SHARD - SPLIT, 64:128].T
+
+
+def call(kernel, out, scratch=(), specs=(VMEM,), out_spec=VMEM, megabytes=8):
     return pl.pallas_call(
         kernel,
         out_shape=out,
-        in_specs=[VMEM] * count,
-        out_specs=jax.tree.map(lambda _: VMEM, out),
+        in_specs=list(specs),
+        out_specs=jax.tree.map(lambda _: out_spec, out),
         scratch_shapes=list(scratch),
-        compiler_params=params(),
+        compiler_params=pltpu.CompilerParams(vmem_limit_bytes=megabytes * 1024 * 1024),
     )
 
 
@@ -200,16 +219,28 @@
 def body(records, positions, weight, cotangent):
     shape = jax.ShapeDtypeStruct
     places = jnp.broadcast_to(positions.astype(BF16)[..., None], positions.shape + (NPOS,))
-    sent = jnp.concatenate([records, places], axis=3).reshape(N_BRICK, 2, REC + NPOS)
-    arrived = spread(sent, "brick").reshape(NPOS, REC + NPOS)
+    sent = call(
+        join_kernel, shape((N_BRICK, 2, REC + NPOS), BF16), [pltpu.SemaphoreType.DMA((9,))],
+        (ANY, ANY), ANY,
+    )(records.reshape(N_BRICK, 2, REC), places.reshape(N_BRICK, 2, NPOS))
+    arrived = spread(sent, BRICK).reshape(NPOS, REC + NPOS)
     full_weight = lax.all_gather(weight, "dp", axis=0, tiled=True)
     wide = call(weight_kernel, shape((TAPS * DEPTH, LINE), BF16))(full_weight)
     arrived, wide = lax.optimization_barrier((arrived, wide))
-    rim = call(rim_kernel, shape((64, 4 * LINE), BF16))(arrived)
-    rim = lax.ppermute(rim, "brick", [(i, i + 1) for i in range(N_BRICK - 1)])
-    activation, terms = call(
+    rim = pl.pallas_call(
+        rim_kernel,
+        out_shape=shape((64, 4 * LINE), BF16),
+        grid=(1,),
+        in_specs=[pl.BlockSpec((NPOS, 13 * 128), lambda _: (0, 0))],
+        out_specs=pl.BlockSpec((64, 4 * LINE), lambda _: (0, 0)),
+        compiler_params=pltpu.CompilerParams(vmem_limit_bytes=8 * 1024 * 1024),
+    )(arrived[:, 12 * LINE :])
+    rim = lax.ppermute(rim, BRICK, [(i, i + 1) for i in range(N_BRICK - 1)])
+    core = lax.axis_index("core").astype(jnp.int32).reshape(1)
+    term = shape((N_CHIP, N_DP * PIECE, 128), F32)
+    activation, kept, given = call(
         layer_kernel,
-        (shape((4, 16, 8 * LINE), BF16), shape((N_BRICK, N_DP * PIECE, 128), BF16)),
+        (shape((4, 16, 8 * LINE), BF16), term, term),
         [
             pltpu.VMEM((4 * NPOS, TAPS * DEPTH), BF16),
             pltpu.VMEM((4 * NPOS, LINE), F32),
@@ -218,27 +249,31 @@
             pltpu.VMEM((4 * NPOS, LINE), BF16),
             pltpu.VMEM((N_DP * ROWS, 128), F32),
         ],
-        4,
-    )(arrived, rim, wide, cotangent.reshape(4, 16, 8 * LINE))
-    sums = call(brick_sum_kernel, shape((N_DP, PIECE, 128), F32))(spread(terms, "brick"))
+        (pl.BlockSpec(memory_space=pltpu.SMEM), VMEM, VMEM, VMEM, VMEM),
+        megabytes=28,
+    )(core, arrived, rim, wide, cotangent.reshape(4, 16, 8 * LINE))
+    taken = lax.ppermute(given, "core", [(0, 1), (1, 0)])
+    terms = spread((kept + taken).astype(BF16), ("x", "y"))
+    sums = call(chip_sum_kernel, shape((N_DP, PIECE, 128), F32))(terms)
     copies = call(scene_sum_kernel, shape((N_BRICK, PIECE, 128), F32))(spread(sums, "dp"))
-    grad = call(unpack_kernel, shape((SHARD, C_OUT), F32), [pltpu.VMEM((ROWS, 128), F32)])(
-        spread(copies, "brick")
-    )
-    return activation.reshape(cotangent.shape), grad
+    grad = call(unpack_kernel, shape((C_OUT, SHARD), F32), [pltpu.VMEM((ROWS, 128), F32)])(
+        spread(copies, BRICK)
+    )
+    return activation.reshape(cotangent.shape), grad.T
 
 
 def solution(mesh):
+    fine = jax.sharding.Mesh(mesh.devices.reshape(N_DP, 4, 8, 2), ("dp", "x", "y", "core"))
     placed = (
-        P(("dp", "brick"), None, None, None),
-        P(("dp", "brick"), None, None),
+        P(("dp",) + BRICK, None, None, None),
+        P(("dp",) + BRICK, None, None),
         P("dp", None),
-        P("dp", "brick", None, None),
+        P("dp", BRICK, None, None),
     )
     return jax.shard_map(
         body,
-        mesh=mesh,
+        mesh=fine,
         in_specs=placed,
-        out_specs=(P("dp", "brick", None, None), P("dp", None)),
+        out_specs=(P("dp", BRICK, None, None), P("dp", None)),
         check_vma=False,
     )

time: 172 us -> 158 us (0.919)
  blocking collectives: 111 us -> 98.5 us
  Pallas kernels: 22.8 us -> 13.9 us
  local copies, waits for them, and re-layouts: 5.68 us -> 12.5 us
  waiting for transfers between devices: 6.17 us -> 10.9 us
  other arithmetic: 4.74 us -> 0.8 us
    all_to_all x3, blocking collectives: 78.8 us -> 66.8 us  [spread(): return lax.all_to_all(block, axis, split_axis=0, concat_axis=0, tiled=True)]
    pallas_call x4 -> x5, Pallas kernels: 17.5 us -> 13.2 us  [the longest x1 9.96 us: body(): call(layer_kernel, (shape((4, 16, 8 * LINE), BF16), term, term), [pltpu.V...]
    reshape x1 -> x0, other arithmetic: 4.05 us -> none  [body(): jnp.concatenate([records, places], axis=3).reshape(N_BRICK, 2, REC + NPOS)]
    reshape x1 -> x2, local copies, waits for them, and re-layouts: 1.51 us -> 4.7 us  [the longest x1 4.57 us: body(): arrived = spread(sent, BRICK).reshape(NPOS, REC + NPOS)]
    pallas_call x1, Pallas kernels: 3.75 us -> 0.68 us  [body(): wide = call(weight_kernel, shape((TAPS * DEPTH, LINE), BF16))(full_weight)]
    ppermute x1 -> x2, waiting for transfers between devices: 2.91 us -> 5.72 us  [the longest x1 2.9 us: body(): rim = lax.ppermute(rim, BRICK, [(i, i + 1) for i in range(N_BRICK - 1)])]
    unnamed x5 -> x10, local copies, waits for them, and re-layouts: 2.41 us -> 5.14 us
    all_to_all x1, waiting for transfers between devices: 3.27 us -> 5.18 us  [spread(): return lax.all_to_all(block, axis, split_axis=0, concat_axis=0, tiled=True)]
  transfers between devices with their start and end apart: 2 -> 3, of which waited for: 2 -> 3; matrix products, arithmetic and copies ran while one was open for 1% -> 1% of each run, Pallas kernels for 2% -> 0%
where the time goes in v2:
time: 158 us
  blocking collectives  98.5 us (62%)
  starting transfers between devices  20.3 us (13%)
  Pallas kernels  13.9 us (9%)
  local copies, waits for them, and re-layouts  12.5 us (8%)
  waiting for transfers between devices  10.9 us (7%)
    all_to_all x3, blocking collectives, spread(): return lax.all_to_all(block, axis, split_axis=0, concat_axis=0, tiled=True)  66.8 us
    all_gather x1, blocking collectives, body(): full_weight = lax.all_gather(weight, 'dp', axis=0, tiled=True)  31.8 us
    all_to_all x1, starting transfers between devices, spread(): return lax.all_to_all(block, axis, split_axis=0, concat_axis=0, tiled=True)  15.5 us
    pallas_call x1, Pallas kernels, body(): call(layer_kernel, (shape((4, 16, 8 * LINE), BF16), term, term), [pltpu.V...  9.96 us
    all_to_all x1, waiting for transfers between devices, spread(): return lax.all_to_all(block, axis, split_axis=0, concat_axis=0, tiled=True)  5.18 us
    unnamed x10, local copies, waits for them, and re-layouts  5.14 us
    reshape x1, local copies, waits for them, and re-layouts, body(): arrived = spread(sent, BRICK).reshape(NPOS, REC + NPOS)  4.57 us
  transfers between devices with their start and end apart: 3, of which 3 were waited for; matrix products, arithmetic and copies ran while one was open for 1% of the time, Pallas kernels for 0%

profile of v2, /device:TPU:1, one launch (start us, length us, event | category | flops | bytes accessed | tf_op | source)
XLA Modules:
  0.0 157.6 jit_solution(6729610594490314328)
XLA Ops:
  0.6 0.7 convert_bitcast_fusion
  1.3 0.1 copy.8
  1.4 0.1 reshape.27.places_ref
  1.6 0.0 copy-start.2
  1.6 1.4 copy-done.2
  3.0 1.2 shard_map.59
  4.2 0.0 copy-start.4
  4.2 15.5 %all-to-all-start = ((bf16[64,2,6272]{2,1,0:T(2,128)(2,1)}), bf16[64,2,6272]{2,1,0:T(2,128)(2,1)}, u32[]{:S(2)}, u32[]{:S(2)}) async-start(bf16[64,2,6272]{2,1,0:T(2,128)(2,1)} %shard_map.59), calls=%async_computation | async-start | bytes 3211264 | tf_op jit(solution)/shard_map/all_to_all | solution.py:216
  19.8 0.0 copy-done.4
  19.8 31.8 %all-gather = bf16[12,216,192]{1,2,0:T(8,128)(2,1)S(1)} all-gather(bf16[1,216,192]{1,2,0:T(8,128)(2,1)S(1)} %bitcast.13), channel_id=1, replica_groups=mesh['dp'=12,'x'=4,'y'=8,'core'=2] {'dp'}, dimensions={0}, use_global_device_ids=true | all-gather | bytes 1078272 | tf_op jit(solution)/shard_map/all_gather | solution.py:227
  51.6 1.5 copy.9
  53.1 0.0 copy-start.1
  53.1 1.3 copy-done.1
  54.4 0.7 shard_map.60.wide_ref
  55.1 5.2 %all-to-all-done = bf16[64,2,6272]{2,1,0:T(2,128)(2,1)} async-done(((bf16[64,2,6272]{2,1,0:T(2,128)(2,1)}), bf16[64,2,6272]{2,1,0:T(2,128)(2,1)}, u32[]{:S(2)}, u32[]{:S(2)}) %all-to-all-start) | async-done | bytes 1605664 | tf_op jit(solution)/shard_map/all_to_all | solution.py:216
  60.3 4.6 %reshape.28.arrived_ref = bf16[128,6272]{1,0:T(8,128)(2,1)} reshape(bf16[64,2,6272]{2,1,0:T(2,128)(2,1)} %all-to-all-done) | data formatting | bytes 3211264 | tf_op jit(solution)/shard_map/reshape | solution.py:226
  64.8 1.0 slice.3.tail_ref
  65.9 0.9 shard_map.61
  66.8 2.9 %collective-permute-start = (bf16[64,1536]{1,0:T(8,128)(2,1)}, bf16[64,1536]{1,0:T(8,128)(2,1)}, u32[]{:S(2)}, u32[]{:S(2)}) collective-permute-start(bf16[64,1536]{1,0:T(8,128)(2,1)} %shard_map.61), channel_id=1, source_target_pairs={{0,1},{1,2},{2,3},{3,4},{4,5},{5,6},{6,7},{7,8},{8,9},{9,10},{10,1... | collective-permute-start | bytes 589832 | tf_op jit(solution)/shard_map/ppermute | solution.py:238
  69.7 2.9 %collective-permute-done.rim_ref = bf16[64,1536]{1,0:T(8,128)(2,1)} collective-permute-done((bf16[64,1536]{1,0:T(8,128)(2,1)}, bf16[64,1536]{1,0:T(8,128)(2,1)}, u32[]{:S(2)}, u32[]{:S(2)}) %collective-permute-start) | collective-permute-done | bytes 196640 | tf_op jit(solution)/shard_map/ppermute | solution.py:238
  72.6 0.0 copy-start
  72.6 1.4 copy-done
  74.0 0.0 copy-start.3
  74.0 1.0 copy-done.3
  75.0 10.0 %shard_map.62 = (bf16[4,16,3072]{2,1,0:T(8,128)(2,1)}, f32[32,72,128]{2,1,0:T(8,128)S(1)}, f32[32,72,128]{2,1,0:T(8,128)S(1)}) custom-call(s32[1]{0:T(128)} %bitcast.core_ref, bf16[128,6272]{1,0:T(8,128)(2,1)S(1)} %copy-done, bf16[64,1536]{1,0:T(8,128)(2,1)} %collective-permute-done.rim_ref, bf16[4608,384]{1,0:T(8,128)(2,1)S(1)} %shard_map.60.wide_ref, ...), custom_call_target="tpu_custom_call" | custom-call | tf_op jit(solution)/shard_map/pallas_call | solution.py:241
  85.0 1.9 %collective-permute-start.1 = (f32[32,72,128]{2,1,0:T(8,128)S(1)}, f32[32,72,128]{2,1,0:T(8,128)S(1)}, u32[]{:S(2)}, u32[]{:S(2)}) collective-permute-start(f32[32,72,128]{2,1,0:T(8,128)S(1)} %get-tuple-element.11), channel_id=1, source_target_pairs={{0,1},{1,0},{2,3},{3,2},{4,5},{5,4},{6,7},{7,6},{8,9},{9,8},{10,11... | collective-permute-start | bytes 3538952 | tf_op jit(solution)/shard_map/ppermute | solution.py:255
  86.9 2.8 %collective-permute-done.1 = f32[32,72,128]{2,1,0:T(8,128)S(1)} collective-permute-done((f32[32,72,128]{2,1,0:T(8,128)S(1)}, f32[32,72,128]{2,1,0:T(8,128)S(1)}, u32[]{:S(2)}, u32[]{:S(2)}) %collective-permute-start.1) | collective-permute-done | bytes 1179680 | tf_op jit(solution)/shard_map/ppermute | solution.py:255
  89.7 0.1 add_convert_fusion
  89.8 27.3 %all_to_all.20.terms_ref = bf16[32,72,128]{2,1,0:T(8,128)(2,1)S(1)} all-to-all(bf16[32,72,128]{2,1,0:T(8,128)(2,1)S(1)} %add_convert_fusion), channel_id=1, replica_groups=mesh['dp'=12,'x'=4,'y'=8,'core'=2] {'x','y'}, dimensions={0} | all-to-all | bytes 1179648 | tf_op jit(solution)/shard_map/all_to_all | solution.py:216
  117.1 0.1 shard_map.63
  117.2 16.8 %all_to_all.21.sums_ref = f32[12,6,128]{2,1,0:T(8,128)S(1)} all-to-all(f32[12,6,128]{2,1,0:T(8,128)S(1)} %shard_map.63), channel_id=1, replica_groups=mesh['dp'=12,'x'=4,'y'=8,'core'=2] {'dp'}, dimensions={0} | all-to-all | bytes 73728 | tf_op jit(solution)/shard_map/all_to_all | solution.py:216
  134.0 22.7 %all_to_all.22.pieces_ref = f32[64,6,128]{2,1,0:T(8,128)S(1)} all-to-all(f32[64,6,128]{2,1,0:T(8,128)S(1)} %shard_map.64), channel_id=1, replica_groups=mesh['dp'=12,'x'=4,'y'=8,'core'=2] {'x','y','core'}, dimensions={0} | all-to-all | bytes 393216 | tf_op jit(solution)/shard_map/all_to_all | solution.py:216
  156.7 0.9 shard_map.65
  (1 shorter events, 0.0 us)
Async XLA Ops:
  1.6 1.4 copy-start.2
  4.2 15.6 %copy-start.4 = (bf16[216,192]{0,1:T(8,128)(2,1)S(1)}, bf16[216,192]{0,1:T(8,128)(2,1)}, u32[]{:S(2)}) copy-start(bf16[216,192]{0,1:T(8,128)(2,1)} %param.6) | copy-start | bytes 248836
  4.2 56.0 %all-to-all-start = ((bf16[64,2,6272]{2,1,0:T(2,128)(2,1)}), bf16[64,2,6272]{2,1,0:T(2,128)(2,1)}, u32[]{:S(2)}, u32[]{:S(2)}) async-start(bf16[64,2,6272]{2,1,0:T(2,128)(2,1)} %shard_map.59), calls=%async_computation | async-start | bytes 3211264 | tf_op jit(solution)/shard_map/all_to_all | solution.py:216
  53.1 1.3 copy-start.1
  66.8 5.8 %collective-permute-start = (bf16[64,1536]{1,0:T(8,128)(2,1)}, bf16[64,1536]{1,0:T(8,128)(2,1)}, u32[]{:S(2)}, u32[]{:S(2)}) collective-permute-start(bf16[64,1536]{1,0:T(8,128)(2,1)} %shard_map.61), channel_id=1, source_target_pairs={{0,1},{1,2},{2,3},{3,4},{4,5},{5,6},{6,7},{7,8},{8,9},{9,10},{10,1... | collective-permute-start | bytes 589832 | tf_op jit(solution)/shard_map/ppermute | solution.py:238
  72.6 1.4 copy-start
  74.0 1.0 copy-start.3
  85.0 4.7 %collective-permute-start.1 = (f32[32,72,128]{2,1,0:T(8,128)S(1)}, f32[32,72,128]{2,1,0:T(8,128)S(1)}, u32[]{:S(2)}, u32[]{:S(2)}) collective-permute-start(f32[32,72,128]{2,1,0:T(8,128)S(1)} %get-tuple-element.11), channel_id=1, source_target_pairs={{0,1},{1,0},{2,3},{3,2},{4,5},{5,4},{6,7},{7,6},{8,9},{9,8},{10,11... | collective-permute-start | bytes 3538952 | tf_op jit(solution)/shard_map/ppermute | solution.py:255

commit v3 on v2

--- a/solution.py
+++ b/solution.py
@@ -20,26 +20,33 @@
 PIECE = 6
 ROWS = N_BRICK * PIECE
 BRICK = ("x", "y", "core")
-ANY = pl.BlockSpec(memory_space=pl.ANY)
+HBM = pl.BlockSpec(memory_space=pltpu.HBM)
 VMEM = pl.BlockSpec(memory_space=pltpu.VMEM)
 F32 = jnp.float32
 BF16 = jnp.bfloat16
 
 
-def join_kernel(records_ref, places_ref, sent_ref, sems):
+def join_kernel(records_ref, positions_ref, sent_ref, rows, tile, sems):
     copies = []
     for part in range(8):
-        rows = pl.ds(part * 8, 8)
+        owners = pl.ds(part * 8, 8)
         copies.append(
             pltpu.make_async_copy(
-                records_ref.at[rows], sent_ref.at[rows, :, pl.ds(0, REC)], sems.at[part]
+                records_ref.at[owners], sent_ref.at[owners, :, pl.ds(0, REC)], sems.at[part]
             )
         )
-    copies.append(
-        pltpu.make_async_copy(places_ref, sent_ref.at[:, :, pl.ds(REC, NPOS)], sems.at[8])
-    )
     for copy in copies:
         copy.start()
+    places = positions_ref[...].astype(F32)
+    for slot in range(2):
+        rows[pl.ds(slot, N_BRICK, stride=2), :] = jnp.broadcast_to(
+            places[slot : slot + 1], (128, N_BRICK)
+        ).T
+    tile[...] = rows[...].astype(BF16).reshape(N_BRICK, 2, NPOS)
+    copies.append(
+        pltpu.make_async_copy(tile, sent_ref.at[:, :, pl.ds(REC, NPOS)], sems.at[8])
+    )
+    copies[8].start()
     for copy in copies:
         copy.wait()
 
@@ -49,29 +56,57 @@
     return q >> 4, (q >> 3) & 1, q & 7
 
 
-def rim_kernel(tail_ref, rim_ref):
-    places = tail_ref[:, 4 * LINE :].astype(F32).T
+def rim_kernel(arrived_ref, rim_ref, tail, sem):
+    copy = pltpu.make_async_copy(arrived_ref.at[:, :, pl.ds(12 * LINE, 13 * 128)], tail, sem)
+    copy.start()
+    copy.wait()
+    places = tail[:, :, 4 * LINE :].reshape(NPOS, NPOS).astype(F32).T
     m = lax.broadcasted_iota(jnp.int32, (64, NPOS), 0)
     wanted = 64 + (m & 7) * 8 + (m >> 3)
     pick = jnp.where(places[:64] == wanted.astype(F32), 1.0, 0.0).astype(BF16)
     rim_ref[...] = jnp.dot(
-        pick, tail_ref[:, 0 : 4 * LINE], preferred_element_type=F32
+        pick, tail[:, :, 0 : 4 * LINE].reshape(NPOS, 4 * LINE), preferred_element_type=F32
     ).astype(BF16)
 
 
 def weight_kernel(weight_ref, wide_ref):
     wide_ref[...] = jnp.zeros_like(wide_ref)
     for tap in range(TAPS):
-        block = weight_ref[tap * 288 : (tap + 1) * 288, :]
+        parts = []
+        start = tap * 288
+        while start < (tap + 1) * 288:
+            d, row = divmod(start, SHARD)
+            size = min((tap + 1) * 288, (d + 1) * SHARD) - start
+            parts.append(weight_ref[d, :, row : row + size])
+            start += size
+        block = jnp.concatenate(parts, axis=1).T
         wide_ref[tap * DEPTH + 32 : tap * DEPTH + 320, 0:C_OUT] = block
         wide_ref[tap * DEPTH + 224 : tap * DEPTH + 512, C_OUT : 2 * C_OUT] = block
 
 
 def layer_kernel(
     core_ref, arrived_ref, rim_ref, wide_ref, cotangent_ref, activation_ref, kept_ref, given_ref,
-    columns, linear, upstream, result, slopes, packed,
+    records, gradient, columns, linear, upstream, result, slopes, packed, sems,
 ):
-    places = arrived_ref[:, REC : REC + NPOS].astype(F32).T
+    copies = []
+    for part, (at, size) in enumerate(
+        [(12 * LINE, 4 * LINE + NPOS), (0, 4 * LINE), (4 * LINE, 4 * LINE), (8 * LINE, 4 * LINE)]
+    ):
+        lanes = pl.ds(at, size)
+        copies.append(
+            pltpu.make_async_copy(
+                arrived_ref.at[:, :, lanes], records.at[:, :, lanes], sems.at[part]
+            )
+        )
+    copies.append(pltpu.make_async_copy(cotangent_ref, gradient, sems.at[4]))
+    for copy in copies:
+        copy.start()
+
+    def part_of(at, size):
+        return records[:, :, at : at + size].reshape(NPOS, size)
+
+    copies[0].wait()
+    places = part_of(REC, NPOS).astype(F32).T
     bz, bx, by = brick_rows((NPOS, NPOS), 0)
     rz, rx, ry = brick_rows((NPOS, 64), 0)
     m = lax.broadcasted_iota(jnp.int32, (NPOS, 64), 1)
@@ -86,7 +121,9 @@
         wanted = jnp.where(inside, (rz - sz) * 8 + ry - sy, -2)
         return jnp.where(m == wanted, 1.0, 0.0).astype(BF16)
 
-    for sx in range(2):
+    for sx in (1, 0):
+        for copy in copies[1:4] if sx == 0 else []:
+            copy.wait()
         for sy in range(2):
             pick = [picker(sx, sy, sz) for sz in range(2)]
             if sx:
@@ -94,10 +131,9 @@
             for vx in [3] if sx else range(4):
                 for vy in [3] if sy else range(4):
                     at = (vx * 4 + vy) * LINE
-                    line = jnp.dot(pick[0], arrived_ref[:, at : at + LINE], preferred_element_type=F32)
-                    before = jnp.dot(
-                        pick[1], arrived_ref[:, at + 256 : at + LINE], preferred_element_type=F32
-                    )
+                    source = part_of(at, LINE)
+                    line = jnp.dot(pick[0], source, preferred_element_type=F32)
+                    before = jnp.dot(pick[1], source[:, 256:], preferred_element_type=F32)
                     if sx:
                         at = vy * LINE
                         line += jnp.dot(
@@ -121,9 +157,10 @@
                                 columns[row : row + NPOS, col + 128 : col + DEPTH] = line
 
     linear[...] = jnp.dot(columns[...], wide_ref[...], preferred_element_type=F32)
+    copies[4].wait()
     for tile in range(24):
         for x in range(4):
-            upstream[x, tile] = cotangent_ref[x, :, tile * 128 : (tile + 1) * 128].astype(F32)
+            upstream[x, tile] = gradient[x, :, tile * 128 : (tile + 1) * 128].astype(F32)
     for i in range(2):
         for j in range(2):
             for z in range(8):
@@ -218,23 +255,27 @@
 
 def body(records, positions, weight, cotangent):
     shape = jax.ShapeDtypeStruct
-    places = jnp.broadcast_to(positions.astype(BF16)[..., None], positions.shape + (NPOS,))
     sent = call(
-        join_kernel, shape((N_BRICK, 2, REC + NPOS), BF16), [pltpu.SemaphoreType.DMA((9,))],
-        (ANY, ANY), ANY,
-    )(records.reshape(N_BRICK, 2, REC), places.reshape(N_BRICK, 2, NPOS))
-    arrived = spread(sent, BRICK).reshape(NPOS, REC + NPOS)
-    full_weight = lax.all_gather(weight, "dp", axis=0, tiled=True)
+        join_kernel,
+        shape((N_BRICK, 2, REC + NPOS), BF16),
+        [
+            pltpu.VMEM((2 * N_BRICK, NPOS), F32),
+            pltpu.VMEM((N_BRICK, 2, NPOS), BF16),
+            pltpu.SemaphoreType.DMA((9,)),
+        ],
+        (HBM, VMEM),
+        HBM,
+    )(records.reshape(N_BRICK, 2, REC), positions.reshape(N_BRICK, 2).T)
+    arrived = spread(sent, BRICK)
+    full_weight = lax.all_gather(weight.T, "dp", axis=0, tiled=False)
     wide = call(weight_kernel, shape((TAPS * DEPTH, LINE), BF16))(full_weight)
     arrived, wide = lax.optimization_barrier((arrived, wide))
-    rim = pl.pallas_call(
+    rim = call(
         rim_kernel,
-        out_shape=shape((64, 4 * LINE), BF16),
-        grid=(1,),
-        in_specs=[pl.BlockSpec((NPOS, 13 * 128), lambda _: (0, 0))],
-        out_specs=pl.BlockSpec((64, 4 * LINE), lambda _: (0, 0)),
-        compiler_params=pltpu.CompilerParams(vmem_limit_bytes=8 * 1024 * 1024),
-    )(arrived[:, 12 * LINE :])
+        shape((64, 4 * LINE), BF16),
+        [pltpu.VMEM((N_BRICK, 2, 13 * 128), BF16), pltpu.SemaphoreType.DMA],
+        (HBM,),
+    )(arrived)
     rim = lax.ppermute(rim, BRICK, [(i, i + 1) for i in range(N_BRICK - 1)])
     core = lax.axis_index("core").astype(jnp.int32).reshape(1)
     term = shape((N_CHIP, N_DP * PIECE, 128), F32)
@@ -242,15 +283,18 @@
         layer_kernel,
         (shape((4, 16, 8 * LINE), BF16), term, term),
         [
+            pltpu.VMEM((N_BRICK, 2, REC + NPOS), BF16),
+            pltpu.VMEM((4, 16, 8 * LINE), BF16),
             pltpu.VMEM((4 * NPOS, TAPS * DEPTH), BF16),
             pltpu.VMEM((4 * NPOS, LINE), F32),
             pltpu.VMEM((4, 24, 16, 128), F32),
             pltpu.VMEM((4, 24, 16, 128), F32),
             pltpu.VMEM((4 * NPOS, LINE), BF16),
             pltpu.VMEM((N_DP * ROWS, 128), F32),
+            pltpu.SemaphoreType.DMA((5,)),
         ],
-        (pl.BlockSpec(memory_space=pltpu.SMEM), VMEM, VMEM, VMEM, VMEM),
-        megabytes=28,
+        (pl.BlockSpec(memory_space=pltpu.SMEM), HBM, VMEM, VMEM, HBM),
+        megabytes=20,
     )(core, arrived, rim, wide, cotangent.reshape(4, 16, 8 * LINE))
     taken = lax.ppermute(given, "core", [(0, 1), (1, 0)])
     terms = spread((kept + taken).astype(BF16), ("x", "y"))

time: 158 us -> 151 us (0.956)
  local copies, waits for them, and re-layouts: 12.5 us -> 5.83 us
    reshape x2 -> x0, local copies, waits for them, and re-layouts: 4.7 us -> none  [the longest x1 4.57 us: body(): arrived = spread(sent, BRICK).reshape(NPOS, REC + NPOS)]
    unnamed x10 -> x12, local copies, waits for them, and re-layouts: 5.14 us -> 5.83 us
  transfers between devices with their start and end apart: 3 -> 3, of which waited for: 3 -> 3; matrix products, arithmetic and copies ran while one was open for 1% -> 0% of each run, Pallas kernels for 0% -> 1%
where the time goes in v3:
time: 151 us; the launch traced here: 150 us
  blocking collectives  98.2 us (65%)
  starting transfers between devices  20.8 us (14%)
  Pallas kernels  14.3 us (9%)
  waiting for transfers between devices  10.2 us (7%)
  local copies, waits for them, and re-layouts  5.83 us (4%)
    all_to_all x3, blocking collectives, spread(): return lax.all_to_all(block, axis, split_axis=0, concat_axis=0, tiled=True)  66.2 us
    all_gather x1, blocking collectives, body(): full_weight = lax.all_gather(weight.T, 'dp', axis=0, tiled=False)  32 us
    all_to_all x1, starting transfers between devices, spread(): return lax.all_to_all(block, axis, split_axis=0, concat_axis=0, tiled=True)  14.8 us
    pallas_call x1, Pallas kernels, body(): call(layer_kernel, (shape((4, 16, 8 * LINE), BF16), term, term), [pltpu.V...  9.69 us
    unnamed x12, local copies, waits for them, and re-layouts  5.83 us
    all_to_all x1, waiting for transfers between devices, spread(): return lax.all_to_all(block, axis, split_axis=0, concat_axis=0, tiled=True)  4.79 us
    ppermute x1, starting transfers between devices, body(): rim = lax.ppermute(rim, BRICK, [(i, i + 1) for i in range(N_BRICK - 1)])  4.09 us
  transfers between devices with their start and end apart: 3, of which 3 were waited for; matrix products, arithmetic and copies ran while one was open for 0% of the time, Pallas kernels for 1%

profile of v3, /device:TPU:1, one launch (start us, length us, event | category | flops | bytes accessed | tf_op | source)
XLA Modules:
  0.0 150.2 jit_solution(7504140399915069237)
XLA Ops:
  0.6 0.0 copy-start.2
  0.6 1.4 copy-done.2
  2.0 0.0 copy-start.4
  2.0 0.7 copy-done.4
  2.7 1.2 shard_map.59
  4.0 0.0 copy-start.5
  4.0 14.8 %all-to-all-start = ((bf16[64,2,6272]{2,1,0:T(2,128)(2,1)}), bf16[64,2,6272]{2,1,0:T(2,128)(2,1)S(1)}, u32[]{:S(2)}, u32[]{:S(2)}) async-start(bf16[64,2,6272]{2,1,0:T(2,128)(2,1)} %shard_map.59), calls=%async_computation | async-start | bytes 3211264 | tf_op jit(solution)/shard_map/all_to_all | solution.py:253
  18.8 0.0 copy-done.5
  18.8 32.0 %all-gather = bf16[2304,216]{1,0:T(8,128)(2,1)S(1)} all-gather(bf16[192,216]{1,0:T(8,128)(2,1)S(1)} %bitcast.15), channel_id=2, replica_groups=mesh['dp'=12,'x'=4,'y'=8,'core'=2] {'dp'}, dimensions={0}, use_global_device_ids=true | all-gather | bytes 1078272 | tf_op jit(solution)/shard_map/all_gather | solution.py:270
  50.8 2.0 %shard_map.60.wide_ref = bf16[4608,384]{1,0:T(8,128)(2,1)S(1)} custom-call(bf16[12,192,216]{2,1,0:T(8,128)(2,1)S(1)} %bitcast.10), custom_call_target="tpu_custom_call" | custom-call | tf_op jit(solution)/shard_map/pallas_call | solution.py:271
  52.8 0.0 copy-start
  52.8 1.7 %copy-done = bf16[4608,384]{1,0:T(8,128)(2,1)} copy-done((bf16[4608,384]{1,0:T(8,128)(2,1)}, bf16[4608,384]{1,0:T(8,128)(2,1)S(1)}, u32[]{:S(2)}) %copy-start) | copy-done | bytes 3538968
  54.5 0.0 copy-start.3
  54.5 4.8 %all-to-all-done.arrived_ref = bf16[64,2,6272]{2,1,0:T(2,128)(2,1)S(1)} async-done(((bf16[64,2,6272]{2,1,0:T(2,128)(2,1)}), bf16[64,2,6272]{2,1,0:T(2,128)(2,1)S(1)}, u32[]{:S(2)}, u32[]{:S(2)}) %all-to-all-start) | async-done | bytes 1605664 | tf_op jit(solution)/shard_map/all_to_all | solution.py:253
  59.3 0.3 shard_map.61
  59.6 4.1 %collective-permute-start = (bf16[64,1536]{1,0:T(8,128)(2,1)S(1)}, bf16[64,1536]{1,0:T(8,128)(2,1)S(1)}, u32[]{:S(2)}, u32[]{:S(2)}) collective-permute-start(bf16[64,1536]{1,0:T(8,128)(2,1)S(1)} %shard_map.61), channel_id=1, source_target_pairs={{0,1},{1,2},{2,3},{3,4},{4,5},{5,6},{6,7},{7,8},{8,9},{9,10},{10,1... | collective-permute-start | bytes 589832 | tf_op jit(solution)/shard_map/ppermute | solution.py:279
  63.7 2.6 %collective-permute-done.rim_ref = bf16[64,1536]{1,0:T(8,128)(2,1)S(1)} collective-permute-done((bf16[64,1536]{1,0:T(8,128)(2,1)S(1)}, bf16[64,1536]{1,0:T(8,128)(2,1)S(1)}, u32[]{:S(2)}, u32[]{:S(2)}) %collective-permute-start) | collective-permute-done | bytes 196640 | tf_op jit(solution)/shard_map/ppermute | solution.py:279
  66.3 0.0 copy-done.3
  66.3 0.0 copy-start.1
  66.3 2.0 %copy-done.1 = bf16[4608,384]{1,0:T(8,128)(2,1)S(1)} copy-done((bf16[4608,384]{1,0:T(8,128)(2,1)S(1)}, bf16[4608,384]{1,0:T(8,128)(2,1)}, u32[]{:S(2)}) %copy-start.1) | copy-done | bytes 3538968
  68.3 9.7 %shard_map.62 = (bf16[4,16,3072]{2,1,0:T(8,128)(2,1)}, f32[32,72,128]{2,1,0:T(8,128)S(1)}, f32[32,72,128]{2,1,0:T(8,128)S(1)}) custom-call(s32[1]{0:T(128)} %bitcast.core_ref, bf16[64,2,6272]{2,1,0:T(2,128)(2,1)S(1)} %all-to-all-done.arrived_ref, bf16[64,1536]{1,0:T(8,128)(2,1)S(1)} %collective-permute-done.rim_ref, bf16[4608,384]{1,0:T(8,128)(2,1)S(1)} %copy-done.1, ...), custom_call_target="tpu_custom_call" | custom-call | tf_op jit(solution)/shard_map/pallas_call | solution.py:282
  78.0 1.9 %collective-permute-start.1 = (f32[32,72,128]{2,1,0:T(8,128)S(1)}, f32[32,72,128]{2,1,0:T(8,128)S(1)}, u32[]{:S(2)}, u32[]{:S(2)}) collective-permute-start(f32[32,72,128]{2,1,0:T(8,128)S(1)} %get-tuple-element.11), channel_id=1, source_target_pairs={{0,1},{1,0},{2,3},{3,2},{4,5},{5,4},{6,7},{7,6},{8,9},{9,8},{10,11... | collective-permute-start | bytes 3538952 | tf_op jit(solution)/shard_map/ppermute | solution.py:299
  79.9 2.8 %collective-permute-done.1 = f32[32,72,128]{2,1,0:T(8,128)S(1)} collective-permute-done((f32[32,72,128]{2,1,0:T(8,128)S(1)}, f32[32,72,128]{2,1,0:T(8,128)S(1)}, u32[]{:S(2)}, u32[]{:S(2)}) %collective-permute-start.1) | collective-permute-done | bytes 1179680 | tf_op jit(solution)/shard_map/ppermute | solution.py:299
  82.8 0.2 add_convert_fusion
  82.9 26.9 %all_to_all.20.terms_ref = bf16[32,72,128]{2,1,0:T(8,128)(2,1)S(1)} all-to-all(bf16[32,72,128]{2,1,0:T(8,128)(2,1)S(1)} %add_convert_fusion), channel_id=1, replica_groups=mesh['dp'=12,'x'=4,'y'=8,'core'=2] {'x','y'}, dimensions={0} | all-to-all | bytes 1179648 | tf_op jit(solution)/shard_map/all_to_all | solution.py:253
  109.8 0.1 shard_map.63
  109.9 16.6 %all_to_all.21.sums_ref = f32[12,6,128]{2,1,0:T(8,128)S(1)} all-to-all(f32[12,6,128]{2,1,0:T(8,128)S(1)} %shard_map.63), channel_id=1, replica_groups=mesh['dp'=12,'x'=4,'y'=8,'core'=2] {'dp'}, dimensions={0} | all-to-all | bytes 73728 | tf_op jit(solution)/shard_map/all_to_all | solution.py:253
  126.5 22.7 %all_to_all.22.pieces_ref = f32[64,6,128]{2,1,0:T(8,128)S(1)} all-to-all(f32[64,6,128]{2,1,0:T(8,128)S(1)} %shard_map.64), channel_id=1, replica_groups=mesh['dp'=12,'x'=4,'y'=8,'core'=2] {'x','y','core'}, dimensions={0} | all-to-all | bytes 393216 | tf_op jit(solution)/shard_map/all_to_all | solution.py:253
  149.2 0.9 shard_map.65
  (1 shorter events, 0.0 us)
Async XLA Ops:
  0.6 1.4 copy-start.2
  2.0 0.7 copy-start.4
  4.0 14.8 %copy-start.5 = (bf16[216,192]{0,1:T(8,128)(2,1)S(1)}, bf16[216,192]{0,1:T(8,128)(2,1)}, u32[]{:S(2)}) copy-start(bf16[216,192]{0,1:T(8,128)(2,1)} %param.6) | copy-start | bytes 248836
  4.0 55.3 %all-to-all-start = ((bf16[64,2,6272]{2,1,0:T(2,128)(2,1)}), bf16[64,2,6272]{2,1,0:T(2,128)(2,1)S(1)}, u32[]{:S(2)}, u32[]{:S(2)}) async-start(bf16[64,2,6272]{2,1,0:T(2,128)(2,1)} %shard_map.59), calls=%async_computation | async-start | bytes 3211264 | tf_op jit(solution)/shard_map/all_to_all | solution.py:253
  52.8 1.8 %copy-start = (bf16[4608,384]{1,0:T(8,128)(2,1)}, bf16[4608,384]{1,0:T(8,128)(2,1)S(1)}, u32[]{:S(2)}) copy-start(bf16[4608,384]{1,0:T(8,128)(2,1)S(1)} %shard_map.60.wide_ref) | copy-start | bytes 10616836
  54.5 11.8 %copy-start.3 = (bf16[1,4,16,3072]{3,2,1,0:T(8,128)(2,1)S(1)}, bf16[1,4,16,3072]{3,2,1,0:T(8,128)(2,1)}, u32[]{:S(2)}) copy-start(bf16[1,4,16,3072]{3,2,1,0:T(8,128)(2,1)} %param.7) | copy-start | bytes 1179652
  59.6 6.7 %collective-permute-start = (bf16[64,1536]{1,0:T(8,128)(2,1)S(1)}, bf16[64,1536]{1,0:T(8,128)(2,1)S(1)}, u32[]{:S(2)}, u32[]{:S(2)}) collective-permute-start(bf16[64,1536]{1,0:T(8,128)(2,1)S(1)} %shard_map.61), channel_id=1, source_target_pairs={{0,1},{1,2},{2,3},{3,4},{4,5},{5,6},{6,7},{7,8},{8,9},{9,10},{10,1... | collective-permute-start | bytes 589832 | tf_op jit(solution)/shard_map/ppermute | solution.py:279
  66.3 2.0 %copy-start.1 = (bf16[4608,384]{1,0:T(8,128)(2,1)S(1)}, bf16[4608,384]{1,0:T(8,128)(2,1)}, u32[]{:S(2)}) copy-start(bf16[4608,384]{1,0:T(8,128)(2,1)} %copy-done) | copy-start | bytes 10616836
  78.0 4.7 %collective-permute-start.1 = (f32[32,72,128]{2,1,0:T(8,128)S(1)}, f32[32,72,128]{2,1,0:T(8,128)S(1)}, u32[]{:S(2)}, u32[]{:S(2)}) collective-permute-start(f32[32,72,128]{2,1,0:T(8,128)S(1)} %get-tuple-element.11), channel_id=1, source_target_pairs={{0,1},{1,0},{2,3},{3,2},{4,5},{5,4},{6,7},{7,6},{8,9},{9,8},{10,11... | collective-permute-start | bytes 3538952 | tf_op jit(solution)/shard_map/ppermute | solution.py:299

commit v4 on v2

v4 whole, which is shorter than its diff:
```python
import jax
import jax.numpy as jnp
from jax import lax
from jax.experimental import pallas as pl
from jax.experimental.pallas import tpu as pltpu
from jax.sharding import PartitionSpec as P

C_IN = 96
C_OUT = 192
REC = 6144
NPOS = 128
LINE = 384
DEPTH = 512
TAPS = 9
N_DP = 12
N_BRICK = 64
N_CHIP = 32
SHARD = 216
SPLIT = 112
PIECE = 6
CHUNKS = 8
ROWS = N_BRICK * PIECE
BRICK = ("x", "y", "core")
HBM = pl.BlockSpec(memory_space=pltpu.HBM)
VMEM = pl.BlockSpec(memory_space=pltpu.VMEM)
F32 = jnp.float32
BF16 = jnp.bfloat16


def join_kernel(records_ref, positions_ref, sent_ref, joined, places, rows, sems):
    size = N_BRICK // CHUNKS
    coming = [pltpu.make_async_copy(positions_ref, places, sems.at[2 * CHUNKS])]
    going = []
    for part in range(CHUNKS):
        owners = pl.ds(part * size, size)
        coming.append(
            pltpu.make_async_copy(
                records_ref.at[owners], joined.at[owners, :, pl.ds(0, REC)], sems.at[part]
            )
        )
        going.append(
            pltpu.make_async_copy(joined.at[owners], sent_ref.at[owners], sems.at[CHUNKS + part])
        )
    for copy in coming:
        copy.start()
    coming[0].wait()
    for slot in range(2):
        rows[pl.ds(slot, N_BRICK, stride=2), :] = jnp.broadcast_to(
            places[slot : slot + 1, :].astype(F32), (128, N_BRICK)
        ).T
    joined[:, :, REC:] = rows[...].astype(BF16).reshape(N_BRICK, 2, NPOS)
    for part in range(CHUNKS):
        coming[1 + part].wait()
        going[part].start()
    for copy in going:
        copy.wait()


def brick_rows(shape, dim):
    q = lax.broadcasted_iota(jnp.int32, shape, dim)
    return q >> 4, (q >> 3) & 1, q & 7


def rim_kernel(arrived_ref, rim_ref):
    places = arrived_ref[:, :, REC:].reshape(NPOS, NPOS).astype(F32).T
    m = lax.broadcasted_iota(jnp.int32, (64, NPOS), 0)
    wanted = 64 + (m & 7) * 8 + (m >> 3)
    pick = jnp.where(places[:64] == wanted.astype(F32), 1.0, 0.0).astype(BF16)
    rim_ref[...] = jnp.dot(
        pick,
        arrived_ref[:, :, 12 * LINE : REC].reshape(NPOS, 4 * LINE),
        preferred_element_type=F32,
    ).astype(BF16)


def widen(weight_ref, wide):
    wide[...] = jnp.zeros_like(wide)
    for tap in range(TAPS):
        parts = []
        start = tap * 288
        while start < (tap + 1) * 288:
            d, row = divmod(start, SHARD)
            size = min((tap + 1) * 288, (d + 1) * SHARD) - start
            parts.append(weight_ref[d, :, row : row + size])
            start += size
        block = jnp.concatenate(parts, axis=1).T
        wide[tap * DEPTH + 32 : tap * DEPTH + 320, 0:C_OUT] = block
        wide[tap * DEPTH + 224 : tap * DEPTH + 512, C_OUT : 2 * C_OUT] = block


def store_line(columns, line, before, ux, uy, width):
    for i in range(2 if width == TAPS else 1):
        for j in range(2):
            a = ux + 1 - 2 * i
            b = uy + 1 - 2 * j
            if 0 <= a <= 2 and 0 <= b <= 2:
                row = (i * 2 + j) * NPOS
                col = (a * 3 + b) * DEPTH
                columns[row : row + NPOS, col : col + 128] = before
                columns[row : row + NPOS, col + 128 : col + DEPTH] = line


def place_kernel(arrived_ref, weight_ref, columns_ref, linear_ref, first_ref, wide):
    widen(weight_ref, wide)
    first_ref[...] = wide[0 : 3 * DEPTH, :]
    places = arrived_ref[:, :, REC:].reshape(NPOS, NPOS).astype(F32).T
    bz, bx, by = brick_rows((NPOS, NPOS), 0)

    def picker(sx, sy, sz):
        inside = (bx >= sx) & (by >= sy) & (bz >= sz)
        wanted = jnp.where(inside, (bx - sx) * 64 + (by - sy) * 8 + bz - sz, -2)
        return jnp.where(places == wanted.astype(F32), 1.0, 0.0).astype(BF16)

    for sx in range(2):
        for sy in range(2):
            pick = [picker(sx, sy, sz) for sz in range(2)]
            for vx in [3] if sx else range(4):
                for vy in [3] if sy else range(4):
                    at = (vx * 4 + vy) * LINE
                    source = arrived_ref[:, :, at : at + LINE].reshape(NPOS, LINE)
                    line = jnp.dot(pick[0], source, preferred_element_type=F32)
                    before = jnp.dot(pick[1], source[:, 256:], preferred_element_type=F32)
                    store_line(
                        columns_ref, line.astype(BF16), before.astype(BF16),
                        vx - 4 * sx, vy - 4 * sy, TAPS,
                    )
    linear_ref[...] = jnp.dot(columns_ref[...], wide[...], preferred_element_type=F32)


def transposed_dot(left, right):
    return lax.dot_general(left, right, (((0,), (0,)), ((), ())), preferred_element_type=F32)


def layer_kernel(
    core_ref, columns_ref, linear_ref, first_ref, rim_ref, cotangent_ref,
    activation_ref, kept_ref, given_ref,
    front, linear, upstream, result, slopes, packed,
):
    rz, rx, ry = brick_rows((NPOS, 64), 0)
    m = lax.broadcasted_iota(jnp.int32, (NPOS, 64), 1)

    def rim_picker(sy, sz):
        inside = (rx == 0) & (ry >= sy) & (rz >= sz)
        wanted = jnp.where(inside, (rz - sz) * 8 + ry - sy, -2)
        return jnp.where(m == wanted, 1.0, 0.0).astype(BF16)

    for sy in range(2):
        pick = [rim_picker(sy, sz) for sz in range(2)]
        for vy in [3] if sy else range(4):
            source = rim_ref[:, vy * LINE : (vy + 1) * LINE]
            line = jnp.dot(pick[0], source, preferred_element_type=F32)
            before = jnp.dot(pick[1], source[:, 256:], preferred_element_type=F32)
            store_line(front, line.astype(BF16), before.astype(BF16), -1, vy - 4 * sy, 3)
    half = 2 * NPOS
    linear[0:half, :] = linear_ref[0:half, :] + jnp.dot(
        front[...], first_ref[...], preferred_element_type=F32
    )
    linear[half:, :] = linear_ref[half:, :]
    front[...] += columns_ref[0:half, 0 : 3 * DEPTH]

    for tile in range(24):
        for x in range(4):
            upstream[x, tile] = cotangent_ref[x, :, tile * 128 : (tile + 1) * 128].astype(F32)
    for i in range(2):
        for j in range(2):
            for z in range(8):
                row = (i * 2 + j) * NPOS + z * 16
                value = linear[row : row + 16, :]
                sigma = 1.0 / (1.0 + jnp.exp(-value))
                active = value * sigma
                slope = sigma * (1.0 + value * (1.0 - sigma))
                incoming = []
                for tile in range(3):
                    lanes = slice(tile * 128, (tile + 1) * 128)
                    parts = []
                    for x in range(2):
                        at = (x * 2 + i, z * 3 + tile, pl.ds(j, 8, stride=2), slice(None))
                        parts.append(upstream[at])
                        result[at] = active[x * 8 : x * 8 + 8, lanes]
                    incoming.append(jnp.concatenate(parts, axis=0))
                incoming = jnp.concatenate(incoming, axis=1)
                slopes[row : row + 16, :] = (incoming * slope).astype(BF16)
    for tile in range(24):
        for x in range(4):
            activation_ref[x, :, tile * 128 : (tile + 1) * 128] = result[x, tile].astype(BF16)

    for d in range(N_DP):
        packed[d * ROWS + SHARD + SPLIT - 8 : (d + 1) * ROWS, :] = jnp.zeros(
            (ROWS - SHARD - SPLIT + 8, 128), F32
        )
    for tap in range(TAPS):
        lanes = slice(tap * DEPTH, (tap + 1) * DEPTH)
        if tap < 3:
            product = transposed_dot(front[:, lanes], slopes[0:half, :]) + transposed_dot(
                columns_ref[half:, lanes], slopes[half:, :]
            )
        else:
            product = transposed_dot(columns_ref[:, lanes], slopes[...])
        block = product[32:320, 0:C_OUT] + product[224:512, C_OUT : 2 * C_OUT]
        start = tap * 288
        while start < (tap + 1) * 288:
            d, row = divmod(start, SHARD)
            stop = min((tap + 1) * 288, d * SHARD + (SPLIT if row < SPLIT else SHARD))
            part = block[start - tap * 288 : stop - tap * 288]
            size = stop - start
            to = d * ROWS + row
            packed[to : to + size, :] = part[:, 0:128]
            if row < SPLIT:
                packed[to + SHARD : to + SHARD + size, 0:64] = part[:, 128:C_OUT]
            else:
                to = to + SHARD - SPLIT
                packed[to : to + size, 64:128] = part[:, 128:C_OUT]
            start = stop
    core = core_ref[0]
    for chip in range(N_CHIP):
        kept_ref[chip] = packed[pl.ds(2 * chip + core, N_DP * PIECE, stride=N_BRICK), :]
        given_ref[chip] = packed[pl.ds(2 * chip + 1 - core, N_DP * PIECE, stride=N_BRICK), :]


def chip_sum_kernel(terms_ref, sums_ref):
    total = terms_ref[0].astype(F32)
    for source in range(1, N_CHIP):
        total += terms_ref[source].astype(F32)
    for d in range(N_DP):
        sums_ref[d] = total[d * PIECE : (d + 1) * PIECE]


def scene_sum_kernel(sums_ref, copies_ref):
    total = sums_ref[0]
    for source in range(1, N_DP):
        total += sums_ref[source]
    for target in range(N_BRICK):
        copies_ref[target] = total


def unpack_kernel(pieces_ref, grad_ref, packed):
    for row in range(PIECE):
        packed[row * N_BRICK : (row + 1) * N_BRICK, :] = pieces_ref[:, row, :]
    grad_ref[0:128, :] = packed[0:SHARD, :].T
    grad_ref[128:C_OUT, 0:SPLIT] = packed[SHARD : SHARD + SPLIT, 0:64].T
    grad_ref[128:C_OUT, SPLIT:SHARD] = packed[SHARD : 2 * SHARD - SPLIT, 64:128].T


def call(kernel, out, scratch=(), specs=(VMEM,), out_spec=VMEM, megabytes=8, flops=0):
    return pl.pallas_call(
        kernel,
        out_shape=out,
        in_specs=list(specs),
        out_specs=jax.tree.map(lambda _: out_spec, out),
        scratch_shapes=list(scratch),
        compiler_params=pltpu.CompilerParams(vmem_limit_bytes=megabytes * 1024 * 1024),
        cost_estimate=pl.CostEstimate(flops=flops, bytes_accessed=0, transcendentals=0) if flops else None,
    )


def spread(block, axis):
    return lax.all_to_all(block, axis, split_axis=0, concat_axis=0, tiled=True)


def body(records, positions, weight, cotangent):
    shape = jax.ShapeDtypeStruct
    sent = call(
        join_kernel,
        shape((N_BRICK, 2, REC + NPOS), BF16),
        [
            pltpu.VMEM((N_BRICK, 2, REC + NPOS), BF16),
            pltpu.VMEM((2, N_BRICK), jnp.int32),
            pltpu.VMEM((2 * N_BRICK, NPOS), F32),
            pltpu.SemaphoreType.DMA((2 * CHUNKS + 1,)),
        ],
        (HBM, HBM),
        HBM,
        61,
    )(records.reshape(N_BRICK, 2, REC), positions.reshape(N_BRICK, 2).T)
    arrived = spread(sent, BRICK)
    full_weight = lax.all_gather(weight.T, "dp", axis=0, tiled=False)
    arrived, full_weight = lax.optimization_barrier((arrived, full_weight))
    rim = call(rim_kernel, shape((64, 4 * LINE), BF16))(arrived)
    rim = lax.ppermute(rim, BRICK, [(i, i + 1) for i in range(N_BRICK - 1)])
    columns, linear, first = call(
        place_kernel,
        (
            shape((4 * NPOS, TAPS * DEPTH), BF16),
            shape((4 * NPOS, LINE), F32),
            shape((3 * DEPTH, LINE), BF16),
        ),
        [pltpu.VMEM((TAPS * DEPTH, LINE), BF16)],
        (VMEM, VMEM),
        megabytes=16,
        flops=2 * 4 * NPOS * TAPS * DEPTH * LINE,
    )(arrived, full_weight)
    core = lax.axis_index("core").astype(jnp.int32).reshape(1)
    term = shape((N_CHIP, N_DP * PIECE, 128), F32)
    activation, kept, given = call(
        layer_kernel,
        (shape((4, 16, 8 * LINE), BF16), term, term),
        [
            pltpu.VMEM((2 * NPOS, 3 * DEPTH), BF16),
            pltpu.VMEM((4 * NPOS, LINE), F32),
            pltpu.VMEM((4, 24, 16, 128), F32),
            pltpu.VMEM((4, 24, 16, 128), F32),
            pltpu.VMEM((4 * NPOS, LINE), BF16),
            pltpu.VMEM((N_DP * ROWS, 128), F32),
        ],
        (pl.BlockSpec(memory_space=pltpu.SMEM),) + (VMEM,) * 5,
        megabytes=16,
    )(core, columns, linear, first, rim, cotangent.reshape(4, 16, 8 * LINE))
    taken = lax.ppermute(given, "core", [(0, 1), (1, 0)])
    terms = spread((kept + taken).astype(BF16), ("x", "y"))
    sums = call(chip_sum_kernel, shape((N_DP, PIECE, 128), F32))(terms)
    copies = call(scene_sum_kernel, shape((N_BRICK, PIECE, 128), F32))(spread(sums, "dp"))
    grad = call(unpack_kernel, shape((C_OUT, SHARD), F32), [pltpu.VMEM((ROWS, 128), F32)])(
        spread(copies, BRICK)
    )
    return activation.reshape(cotangent.shape), grad.T


def solution(mesh):
    fine = jax.sharding.Mesh(mesh.devices.reshape(N_DP, 4, 8, 2), ("dp", "x", "y", "core"))
    placed = (
        P(("dp",) + BRICK, None, None, None),
        P(("dp",) + BRICK, None, None),
        P("dp", None),
        P("dp", BRICK, None, None),
    )
    return jax.shard_map(
        body,
        mesh=fine,
        in_specs=placed,
        out_specs=(P("dp", BRICK, None, None), P("dp", None)),
        check_vma=False,
    )
```

time: 158 us -> 144 us (0.911)
  local copies, waits for them, and re-layouts: 12.5 us -> 0.01 us
    unnamed x10 -> x4, local copies, waits for them, and re-layouts: 5.14 us -> 0.01 us
    reshape x2 -> x0, local copies, waits for them, and re-layouts: 4.7 us -> none  [the longest x1 4.57 us: body(): arrived = spread(sent, BRICK).reshape(NPOS, REC + NPOS)]
    pallas_call x3, Pallas kernels: 2.85 us -> 6.75 us  [the longest x1 4.14 us: body(): call(place_kernel, (shape((4 * NPOS, TAPS * DEPTH), BF16), shape((4 * NPO...]
    pallas_call x1, Pallas kernels: 9.96 us -> 6.19 us  [body(): call(layer_kernel, (shape((4, 16, 8 * LINE), BF16), term, term), [pltpu.V...]
    all_to_all x1, waiting for transfers between devices: 5.18 us -> 8.53 us  [spread(): return lax.all_to_all(block, axis, split_axis=0, concat_axis=0, tiled=True)]
    ppermute x1, waiting for transfers between devices: 2.9 us -> 0.01 us  [body(): rim = lax.ppermute(rim, BRICK, [(i, i + 1) for i in range(N_BRICK - 1)])]
  transfers between devices with their start and end apart: 3 -> 3, of which waited for: 3 -> 2; matrix products, arithmetic and copies ran while one was open for 1% -> 0% of each run, Pallas kernels for 0% -> 3%
where the time goes in v4:
time: 144 us
  blocking collectives  97.8 us (68%)
  starting transfers between devices  19.5 us (14%)
  Pallas kernels  14 us (10%)
  waiting for transfers between devices  11.3 us (8%)
    all_to_all x3, blocking collectives, spread(): return lax.all_to_all(block, axis, split_axis=0, concat_axis=0, tiled=True)  65.8 us
    all_gather x1, blocking collectives, body(): full_weight = lax.all_gather(weight.T, 'dp', axis=0, tiled=False)  32 us
    all_to_all x1, starting transfers between devices, spread(): return lax.all_to_all(block, axis, split_axis=0, concat_axis=0, tiled=True)  14.8 us
    all_to_all x1, waiting for transfers between devices, spread(): return lax.all_to_all(block, axis, split_axis=0, concat_axis=0, tiled=True)  8.53 us
    pallas_call x1, Pallas kernels, body(): call(layer_kernel, (shape((4, 16, 8 * LINE), BF16), term, term), [pltpu.V...  6.19 us
    pallas_call x1, Pallas kernels, body(): call(place_kernel, (shape((4 * NPOS, TAPS * DEPTH), BF16), shape((4 * NPO...  4.14 us
  transfers between devices with their start and end apart: 3, of which 2 were waited for; matrix products, arithmetic and copies ran while one was open for 0% of the time, Pallas kernels for 3%

profile of v4, /device:TPU:1, one launch (start us, length us, event | category | flops | bytes accessed | tf_op | source)
XLA Modules:
  0.0 143.5 jit_solution(15993153233268808042)
XLA Ops:
  0.6 2.4 %shard_map.59 = bf16[64,2,6272]{2,1,0:T(2,128)(2,1)} custom-call(bf16[64,2,6144]{2,1,0:T(2,128)(2,1)} %bitcast.12, s32[2,64]{1,0:T(2,128)} %bitcast.15), custom_call_target="tpu_custom_call" | custom-call | tf_op jit(solution)/shard_map/pallas_call | solution.py:262
  3.0 0.0 copy-start.1
  3.0 14.8 %all-to-all-start = ((bf16[64,2,6272]{2,1,0:T(2,128)(2,1)}), bf16[64,2,6272]{2,1,0:T(2,128)(2,1)S(1)}, u32[]{:S(2)}, u32[]{:S(2)}) async-start(bf16[64,2,6272]{2,1,0:T(2,128)(2,1)} %shard_map.59), calls=%async_computation | async-start | bytes 3211264 | tf_op jit(solution)/shard_map/all_to_all | solution.py:257
  17.8 0.0 copy-done.1
  17.8 32.0 %all-gather = bf16[2304,216]{1,0:T(8,128)(2,1)S(1)} all-gather(bf16[192,216]{1,0:T(8,128)(2,1)S(1)} %bitcast.14), channel_id=2, replica_groups=mesh['dp'=12,'x'=4,'y'=8,'core'=2] {'dp'}, dimensions={0}, use_global_device_ids=true | all-gather | bytes 1078272 | tf_op jit(solution)/shard_map/all_gather | solution.py:276
  49.8 8.5 %all-to-all-done.arrived_ref = bf16[64,2,6272]{2,1,0:T(2,128)(2,1)S(1)} async-done(((bf16[64,2,6272]{2,1,0:T(2,128)(2,1)}), bf16[64,2,6272]{2,1,0:T(2,128)(2,1)S(1)}, u32[]{:S(2)}, u32[]{:S(2)}) %all-to-all-start) | async-done | bytes 1605664 | tf_op jit(solution)/shard_map/all_to_all | solution.py:257
  58.3 0.3 shard_map.61
  58.6 2.9 %collective-permute-start = (bf16[64,1536]{1,0:T(8,128)(2,1)S(1)}, bf16[64,1536]{1,0:T(8,128)(2,1)S(1)}, u32[]{:S(2)}, u32[]{:S(2)}) collective-permute-start(bf16[64,1536]{1,0:T(8,128)(2,1)S(1)} %shard_map.61), channel_id=1, source_target_pairs={{0,1},{1,2},{2,3},{3,4},{4,5},{5,6},{6,7},{7,8},{8,9},{9,10},{10,1... | collective-permute-start | bytes 589832 | tf_op jit(solution)/shard_map/ppermute | solution.py:279
  61.5 0.0 copy-start
  61.5 4.1 %shard_map.60 = (bf16[512,4608]{1,0:T(8,128)(2,1)S(1)}, f32[512,384]{1,0:T(8,128)S(1)}, bf16[1536,384]{1,0:T(8,128)(2,1)S(1)}) custom-call(bf16[64,2,6272]{2,1,0:T(2,128)(2,1)S(1)} %all-to-all-done.arrived_ref, bf16[12,192,216]{2,1,0:T(8,128)(2,1)S(1)} %bitcast.10), custom_call_target="tpu_custom_call" | custom-call | flops 1811939328 | tf_op jit(solution)/shard_map/pallas_call | solution.py:280
  65.6 0.0 collective-permute-done.rim_ref
  65.6 0.0 copy-done
  65.6 6.2 %shard_map.62 = (bf16[4,16,3072]{2,1,0:T(8,128)(2,1)}, f32[32,72,128]{2,1,0:T(8,128)S(1)}, f32[32,72,128]{2,1,0:T(8,128)S(1)}) custom-call(s32[1]{0:T(128)} %bitcast.core_ref, bf16[512,4608]{1,0:T(8,128)(2,1)S(1)} %get-tuple-element.12.columns_ref, f32[512,384]{1,0:T(8,128)S(1)} %get-tuple-element.13.linear_ref, ...), custom_call_target="tpu_custom_call" | custom-call | tf_op jit(solution)/shard_map/pallas_call | solution.py:294
  71.8 1.9 %collective-permute-start.1 = (f32[32,72,128]{2,1,0:T(8,128)S(1)}, f32[32,72,128]{2,1,0:T(8,128)S(1)}, u32[]{:S(2)}, u32[]{:S(2)}) collective-permute-start(f32[32,72,128]{2,1,0:T(8,128)S(1)} %get-tuple-element.17), channel_id=1, source_target_pairs={{0,1},{1,0},{2,3},{3,2},{4,5},{5,4},{6,7},{7,6},{8,9},{9,8},{10,11... | collective-permute-start | bytes 3538952 | tf_op jit(solution)/shard_map/ppermute | solution.py:308
  73.8 2.8 %collective-permute-done.1 = f32[32,72,128]{2,1,0:T(8,128)S(1)} collective-permute-done((f32[32,72,128]{2,1,0:T(8,128)S(1)}, f32[32,72,128]{2,1,0:T(8,128)S(1)}, u32[]{:S(2)}, u32[]{:S(2)}) %collective-permute-start.1) | collective-permute-done | bytes 1179680 | tf_op jit(solution)/shard_map/ppermute | solution.py:308
  76.6 0.1 add_convert_fusion
  76.7 22.8 %all_to_all.20.terms_ref = bf16[32,72,128]{2,1,0:T(8,128)(2,1)S(1)} all-to-all(bf16[32,72,128]{2,1,0:T(8,128)(2,1)S(1)} %add_convert_fusion), channel_id=1, replica_groups=mesh['dp'=12,'x'=4,'y'=8,'core'=2] {'x','y'}, dimensions={0} | all-to-all | bytes 1179648 | tf_op jit(solution)/shard_map/all_to_all | solution.py:257
  99.5 0.1 shard_map.63
  99.6 20.3 %all_to_all.21.sums_ref = f32[12,6,128]{2,1,0:T(8,128)S(1)} all-to-all(f32[12,6,128]{2,1,0:T(8,128)S(1)} %shard_map.63), channel_id=1, replica_groups=mesh['dp'=12,'x'=4,'y'=8,'core'=2] {'dp'}, dimensions={0} | all-to-all | bytes 73728 | tf_op jit(solution)/shard_map/all_to_all | solution.py:257
  119.9 22.7 %all_to_all.22.pieces_ref = f32[64,6,128]{2,1,0:T(8,128)S(1)} all-to-all(f32[64,6,128]{2,1,0:T(8,128)S(1)} %shard_map.64), channel_id=1, replica_groups=mesh['dp'=12,'x'=4,'y'=8,'core'=2] {'x','y','core'}, dimensions={0} | all-to-all | bytes 393216 | tf_op jit(solution)/shard_map/all_to_all | solution.py:257
  142.6 0.9 shard_map.65
  (1 shorter events, 0.0 us)
Async XLA Ops:
  3.0 14.8 %copy-start.1 = (bf16[216,192]{0,1:T(8,128)(2,1)S(1)}, bf16[216,192]{0,1:T(8,128)(2,1)}, u32[]{:S(2)}) copy-start(bf16[216,192]{0,1:T(8,128)(2,1)} %param.6) | copy-start | bytes 248836
  3.0 55.3 %all-to-all-start = ((bf16[64,2,6272]{2,1,0:T(2,128)(2,1)}), bf16[64,2,6272]{2,1,0:T(2,128)(2,1)S(1)}, u32[]{:S(2)}, u32[]{:S(2)}) async-start(bf16[64,2,6272]{2,1,0:T(2,128)(2,1)} %shard_map.59), calls=%async_computation | async-start | bytes 3211264 | tf_op jit(solution)/shard_map/all_to_all | solution.py:257
  58.6 7.0 %collective-permute-start = (bf16[64,1536]{1,0:T(8,128)(2,1)S(1)}, bf16[64,1536]{1,0:T(8,128)(2,1)S(1)}, u32[]{:S(2)}, u32[]{:S(2)}) collective-permute-start(bf16[64,1536]{1,0:T(8,128)(2,1)S(1)} %shard_map.61), channel_id=1, source_target_pairs={{0,1},{1,2},{2,3},{3,4},{4,5},{5,6},{6,7},{7,8},{8,9},{9,10},{10,1... | collective-permute-start | bytes 589832 | tf_op jit(solution)/shard_map/ppermute | solution.py:279
  61.5 4.2 %copy-start = (bf16[1,4,16,3072]{3,2,1,0:T(8,128)(2,1)S(1)}, bf16[1,4,16,3072]{3,2,1,0:T(8,128)(2,1)}, u32[]{:S(2)}) copy-start(bf16[1,4,16,3072]{3,2,1,0:T(8,128)(2,1)} %param.7) | copy-start | bytes 1179652
  71.8 4.7 %collective-permute-start.1 = (f32[32,72,128]{2,1,0:T(8,128)S(1)}, f32[32,72,128]{2,1,0:T(8,128)S(1)}, u32[]{:S(2)}, u32[]{:S(2)}) collective-permute-start(f32[32,72,128]{2,1,0:T(8,128)S(1)} %get-tuple-element.17), channel_id=1, source_target_pairs={{0,1},{1,0},{2,3},{3,2},{4,5},{5,4},{6,7},{7,6},{8,9},{9,8},{10,11... | collective-permute-start | bytes 3538952 | tf_op jit(solution)/shard_map/ppermute | solution.py:308

commit v5 on v4

--- a/solution.py
+++ b/solution.py
@@ -17,8 +17,11 @@
 N_CHIP = 32
 SHARD = 216
 SPLIT = 112
-PIECE = 6
+KEEP = 104
+PIECE = 5
+TERM = 64
 CHUNKS = 8
+WIDTH = (PIECE + 1) * 128
 ROWS = N_BRICK * PIECE
 BRICK = ("x", "y", "core")
 HBM = pl.BlockSpec(memory_space=pltpu.HBM)
@@ -27,7 +30,7 @@
 BF16 = jnp.bfloat16
 
 
-def join_kernel(records_ref, positions_ref, sent_ref, joined, places, rows, sems):
+def join_kernel(records_ref, positions_ref, sent_ref, staged, tile, places, rows, sems):
     size = N_BRICK // CHUNKS
     coming = [pltpu.make_async_copy(positions_ref, places, sems.at[2 * CHUNKS])]
     going = []
@@ -35,20 +38,28 @@
         owners = pl.ds(part * size, size)
         coming.append(
             pltpu.make_async_copy(
-                records_ref.at[owners], joined.at[owners, :, pl.ds(0, REC)], sems.at[part]
+                records_ref.at[owners], staged.at[owners], sems.at[part]
             )
         )
         going.append(
-            pltpu.make_async_copy(joined.at[owners], sent_ref.at[owners], sems.at[CHUNKS + part])
+            pltpu.make_async_copy(
+                staged.at[owners], sent_ref.at[owners, :, pl.ds(0, REC)], sems.at[CHUNKS + part]
+            )
         )
     for copy in coming:
         copy.start()
+    going.append(
+        pltpu.make_async_copy(
+            tile, sent_ref.at[:, :, pl.ds(REC, NPOS)], sems.at[2 * CHUNKS + 1]
+        )
+    )
     coming[0].wait()
     for slot in range(2):
         rows[pl.ds(slot, N_BRICK, stride=2), :] = jnp.broadcast_to(
             places[slot : slot + 1, :].astype(F32), (128, N_BRICK)
         ).T
-    joined[:, :, REC:] = rows[...].astype(BF16).reshape(N_BRICK, 2, NPOS)
+    tile[...] = rows[...].astype(BF16).reshape(N_BRICK, 2, NPOS)
+    going[CHUNKS].start()
     for part in range(CHUNKS):
         coming[1 + part].wait()
         going[part].start()
@@ -73,8 +84,7 @@
     ).astype(BF16)
 
 
-def widen(weight_ref, wide):
-    wide[...] = jnp.zeros_like(wide)
+def weight_kernel(weight_ref, tall_ref):
     for tap in range(TAPS):
         parts = []
         start = tap * 288
@@ -83,9 +93,18 @@
             size = min((tap + 1) * 288, (d + 1) * SHARD) - start
             parts.append(weight_ref[d, :, row : row + size])
             start += size
-        block = jnp.concatenate(parts, axis=1).T
-        wide[tap * DEPTH + 32 : tap * DEPTH + 320, 0:C_OUT] = block
-        wide[tap * DEPTH + 224 : tap * DEPTH + 512, C_OUT : 2 * C_OUT] = block
+        tall_ref[tap * 288 : (tap + 1) * 288, :] = jnp.concatenate(parts, axis=1).T
+
+
+def widen(tall_ref, wide):
+    for tap in range(TAPS):
+        at = tap * DEPTH
+        block = tall_ref[tap * 288 : (tap + 1) * 288, :]
+        wide[at : at + 32, 0:C_OUT] = jnp.zeros((32, C_OUT), BF16)
+        wide[at + 32 : at + 320, 0:C_OUT] = block
+        wide[at + 320 : at + 512, 0:C_OUT] = jnp.zeros((192, C_OUT), BF16)
+        wide[at : at + 224, C_OUT:] = jnp.zeros((224, C_OUT), BF16)
+        wide[at + 224 : at + 512, C_OUT:] = block
 
 
 def store_line(columns, line, before, ux, uy, width):
@@ -100,8 +119,8 @@
                 columns[row : row + NPOS, col + 128 : col + DEPTH] = line
 
 
-def place_kernel(arrived_ref, weight_ref, columns_ref, linear_ref, first_ref, wide):
-    widen(weight_ref, wide)
+def place_kernel(arrived_ref, tall_ref, columns_ref, linear_ref, first_ref, wide):
+    widen(tall_ref, wide)
     first_ref[...] = wide[0 : 3 * DEPTH, :]
     places = arrived_ref[:, :, REC:].reshape(NPOS, NPOS).astype(F32).T
     bz, bx, by = brick_rows((NPOS, NPOS), 0)
@@ -127,14 +146,10 @@
     linear_ref[...] = jnp.dot(columns_ref[...], wide[...], preferred_element_type=F32)
 
 
-def transposed_dot(left, right):
-    return lax.dot_general(left, right, (((0,), (0,)), ((), ())), preferred_element_type=F32)
-
-
 def layer_kernel(
     core_ref, columns_ref, linear_ref, first_ref, rim_ref, cotangent_ref,
     activation_ref, kept_ref, given_ref,
-    front, linear, upstream, result, slopes, packed,
+    front, linear, upstream, result, slopes, packed, left, turned_left,
 ):
     rz, rx, ry = brick_rows((NPOS, 64), 0)
     m = lax.broadcasted_iota(jnp.int32, (NPOS, 64), 1)
@@ -179,50 +194,66 @@
                         result[at] = active[x * 8 : x * 8 + 8, lanes]
                     incoming.append(jnp.concatenate(parts, axis=0))
                 incoming = jnp.concatenate(incoming, axis=1)
-                slopes[row : row + 16, :] = (incoming * slope).astype(BF16)
+                change = (incoming * slope).astype(BF16)
+                slopes[0, row : row + 16, :] = change[:, 0:C_OUT]
+                slopes[1, row : row + 16, :] = change[:, C_OUT:]
     for tile in range(24):
         for x in range(4):
             activation_ref[x, :, tile * 128 : (tile + 1) * 128] = result[x, tile].astype(BF16)
 
-    for d in range(N_DP):
-        packed[d * ROWS + SHARD + SPLIT - 8 : (d + 1) * ROWS, :] = jnp.zeros(
-            (ROWS - SHARD - SPLIT + 8, 128), F32
-        )
+    left[:, 64:128] = jnp.zeros((N_DP * 8, 64), F32)
+    turned_left[:, N_DP * 8 :] = jnp.zeros((NPOS, NPOS - N_DP * 8), F32)
     for tap in range(TAPS):
         lanes = slice(tap * DEPTH, (tap + 1) * DEPTH)
         if tap < 3:
-            product = transposed_dot(front[:, lanes], slopes[0:half, :]) + transposed_dot(
-                columns_ref[half:, lanes], slopes[half:, :]
-            )
+            turned = jnp.concatenate([front[:, lanes], columns_ref[half:, lanes]], axis=0).T
         else:
-            product = transposed_dot(columns_ref[:, lanes], slopes[...])
-        block = product[32:320, 0:C_OUT] + product[224:512, C_OUT : 2 * C_OUT]
+            turned = columns_ref[:, lanes].T
+        product = [
+            jnp.dot(turned[k * 128 : k * 128 + 384], slopes[k], preferred_element_type=F32)
+            for k in range(2)
+        ]
+        block = product[0][32:320] + product[1][96:384]
         start = tap * 288
         while start < (tap + 1) * 288:
             d, row = divmod(start, SHARD)
-            stop = min((tap + 1) * 288, d * SHARD + (SPLIT if row < SPLIT else SHARD))
+            limit = KEEP if row < KEEP else SPLIT if row < SPLIT else SHARD
+            stop = min((tap + 1) * 288, d * SHARD + limit)
             part = block[start - tap * 288 : stop - tap * 288]
             size = stop - start
             to = d * ROWS + row
             packed[to : to + size, :] = part[:, 0:128]
-            if row < SPLIT:
+            if row < KEEP:
                 packed[to + SHARD : to + SHARD + size, 0:64] = part[:, 128:C_OUT]
+            elif row < SPLIT:
+                to = d * 8 + row - KEEP
+                left[to : to + size, 0:64] = part[:, 128:C_OUT]
             else:
                 to = to + SHARD - SPLIT
                 packed[to : to + size, 64:128] = part[:, 128:C_OUT]
             start = stop
+    turned_left[:, 0 : N_DP * 8] = left[...].T
     core = core_ref[0]
+    rows = N_DP * PIECE
     for chip in range(N_CHIP):
-        kept_ref[chip] = packed[pl.ds(2 * chip + core, N_DP * PIECE, stride=N_BRICK), :]
-        given_ref[chip] = packed[pl.ds(2 * chip + 1 - core, N_DP * PIECE, stride=N_BRICK), :]
+        for target, piece in ((kept_ref, 2 * chip + core), (given_ref, 2 * chip + 1 - core)):
+            target[chip, 0:rows, :] = packed[pl.ds(piece, rows, stride=N_BRICK), :]
+            target[chip, rows : rows + 1, :] = turned_left[pl.ds(piece, 1), :]
+            target[chip, rows + 1 :, :] = jnp.zeros((TERM - rows - 1, 128), F32)
 
 
 def chip_sum_kernel(terms_ref, sums_ref):
     total = terms_ref[0].astype(F32)
     for source in range(1, N_CHIP):
         total += terms_ref[source].astype(F32)
+    last = N_DP * PIECE
     for d in range(N_DP):
-        sums_ref[d] = total[d * PIECE : (d + 1) * PIECE]
+        for row in range(PIECE):
+            at = d * PIECE + row
+            sums_ref[d, :, row * 128 : (row + 1) * 128] = total[at : at + 1]
+        sums_ref[d, :, PIECE * 128 :] = jnp.concatenate(
+            [total[last : last + 1, d * 8 : d * 8 + 8], jnp.zeros((1, 120), F32)], axis=1
+        )
 
 
 def scene_sum_kernel(sums_ref, copies_ref):
@@ -235,10 +266,13 @@
 
 def unpack_kernel(pieces_ref, grad_ref, packed):
     for row in range(PIECE):
-        packed[row * N_BRICK : (row + 1) * N_BRICK, :] = pieces_ref[:, row, :]
+        packed[row * N_BRICK : (row + 1) * N_BRICK, :] = pieces_ref[
+            :, 0, row * 128 : (row + 1) * 128
+        ]
     grad_ref[0:128, :] = packed[0:SHARD, :].T
-    grad_ref[128:C_OUT, 0:SPLIT] = packed[SHARD : SHARD + SPLIT, 0:64].T
-    grad_ref[128:C_OUT, SPLIT:SHARD] = packed[SHARD : 2 * SHARD - SPLIT, 64:128].T
+    grad_ref[128:C_OUT, 0:KEEP] = packed[SHARD : SHARD + KEEP, 0:64].T
+    grad_ref[128:C_OUT, KEEP:SPLIT] = pieces_ref[:, 0, PIECE * 128 : PIECE * 128 + 128][:, 0:8]
+    grad_ref[128:C_OUT, SPLIT:SHARD] = packed[SHARD : SHARD + KEEP, 64:128].T
 
 
 def call(kernel, out, scratch=(), specs=(VMEM,), out_spec=VMEM, megabytes=8, flops=0):
@@ -263,10 +297,11 @@
         join_kernel,
         shape((N_BRICK, 2, REC + NPOS), BF16),
         [
-            pltpu.VMEM((N_BRICK, 2, REC + NPOS), BF16),
+            pltpu.VMEM((N_BRICK, 2, REC), BF16),
+            pltpu.VMEM((N_BRICK, 2, NPOS), BF16),
             pltpu.VMEM((2, N_BRICK), jnp.int32),
             pltpu.VMEM((2 * N_BRICK, NPOS), F32),
-            pltpu.SemaphoreType.DMA((2 * CHUNKS + 1,)),
+            pltpu.SemaphoreType.DMA((2 * CHUNKS + 2,)),
         ],
         (HBM, HBM),
         HBM,
@@ -274,7 +309,8 @@
     )(records.reshape(N_BRICK, 2, REC), positions.reshape(N_BRICK, 2).T)
     arrived = spread(sent, BRICK)
     full_weight = lax.all_gather(weight.T, "dp", axis=0, tiled=False)
-    arrived, full_weight = lax.optimization_barrier((arrived, full_weight))
+    tall = call(weight_kernel, shape((TAPS * 288, C_OUT), BF16))(full_weight)
+    arrived, tall = lax.optimization_barrier((arrived, tall))
     rim = call(rim_kernel, shape((64, 4 * LINE), BF16))(arrived)
     rim = lax.ppermute(rim, BRICK, [(i, i + 1) for i in range(N_BRICK - 1)])
     columns, linear, first = call(
@@ -288,9 +324,9 @@
         (VMEM, VMEM),
         megabytes=16,
         flops=2 * 4 * NPOS * TAPS * DEPTH * LINE,
-    )(arrived, full_weight)
+    )(arrived, tall)
     core = lax.axis_index("core").astype(jnp.int32).reshape(1)
-    term = shape((N_CHIP, N_DP * PIECE, 128), F32)
+    term = shape((N_CHIP, TERM, 128), F32)
     activation, kept, given = call(
         layer_kernel,
         (shape((4, 16, 8 * LINE), BF16), term, term),
@@ -299,16 +335,18 @@
             pltpu.VMEM((4 * NPOS, LINE), F32),
             pltpu.VMEM((4, 24, 16, 128), F32),
             pltpu.VMEM((4, 24, 16, 128), F32),
-            pltpu.VMEM((4 * NPOS, LINE), BF16),
-            pltpu.VMEM((N_DP * ROWS, 128), F32),
+            pltpu.VMEM((2, 4 * NPOS, C_OUT), BF16),
+            pltpu.VMEM((TERM * N_BRICK, 128), F32),
+            pltpu.VMEM((N_DP * 8, 128), F32),
+            pltpu.VMEM((NPOS, NPOS), F32),
         ],
         (pl.BlockSpec(memory_space=pltpu.SMEM),) + (VMEM,) * 5,
         megabytes=16,
     )(core, columns, linear, first, rim, cotangent.reshape(4, 16, 8 * LINE))
     taken = lax.ppermute(given, "core", [(0, 1), (1, 0)])
     terms = spread((kept + taken).astype(BF16), ("x", "y"))
-    sums = call(chip_sum_kernel, shape((N_DP, PIECE, 128), F32))(terms)
-    copies = call(scene_sum_kernel, shape((N_BRICK, PIECE, 128), F32))(spread(sums, "dp"))
+    sums = call(chip_sum_kernel, shape((N_DP, 1, WIDTH), F32))(terms)
+    copies = call(scene_sum_kernel, shape((N_BRICK, 1, WIDTH), F32))(spread(sums, "dp"))
     grad = call(unpack_kernel, shape((C_OUT, SHARD), F32), [pltpu.VMEM((ROWS, 128), F32)])(
         spread(copies, BRICK)
     )

time: 144 us -> 140 us (0.972)
  blocking collectives: 97.8 us -> 95.2 us
    all_to_all x3, blocking collectives: 65.8 us -> 63.2 us  [spread(): return lax.all_to_all(block, axis, split_axis=0, concat_axis=0, tiled=True)]
  transfers between devices with their start and end apart: 3 -> 3, of which waited for: 2 -> 2; matrix products, arithmetic and copies ran while one was open for 0% -> 0% of each run, Pallas kernels for 3% -> 4%
where the time goes in v5:
time: 140 us
  blocking collectives  95.2 us (68%)
  starting transfers between devices  19.6 us (14%)
  Pallas kernels  14.1 us (10%)
  waiting for transfers between devices  10.2 us (7%)
    all_to_all x3, blocking collectives, spread(): return lax.all_to_all(block, axis, split_axis=0, concat_axis=0, tiled=True)  63.2 us
    all_gather x1, blocking collectives, body(): full_weight = lax.all_gather(weight.T, 'dp', axis=0, tiled=False)  32 us
    all_to_all x1, starting transfers between devices, spread(): return lax.all_to_all(block, axis, split_axis=0, concat_axis=0, tiled=True)  14.8 us
    all_to_all x1, waiting for transfers between devices, spread(): return lax.all_to_all(block, axis, split_axis=0, concat_axis=0, tiled=True)  7.61 us
    pallas_call x1, Pallas kernels, body(): call(layer_kernel, (shape((4, 16, 8 * LINE), BF16), term, term), [pltpu.V...  5.45 us
    pallas_call x1, Pallas kernels, body(): call(place_kernel, (shape((4 * NPOS, TAPS * DEPTH), BF16), shape((4 * NPO...  4.01 us
    ppermute x1, starting transfers between devices, body(): rim = lax.ppermute(rim, BRICK, [(i, i + 1) for i in range(N_BRICK - 1)])  2.88 us
  transfers between devices with their start and end apart: 3, of which 2 were waited for; matrix products, arithmetic and copies ran while one was open for 0% of the time, Pallas kernels for 4%

profile of v5, /device:TPU:1, one launch (start us, length us, event | category | flops | bytes accessed | tf_op | source)
XLA Modules:
  0.0 140.0 jit_solution(15238429263030404847)
XLA Ops:
  0.6 2.4 %shard_map.59 = bf16[64,2,6272]{2,1,0:T(2,128)(2,1)} custom-call(bf16[64,2,6144]{2,1,0:T(2,128)(2,1)} %bitcast.12, s32[2,64]{1,0:T(2,128)} %bitcast.15), custom_call_target="tpu_custom_call" | custom-call | tf_op jit(solution)/shard_map/pallas_call | solution.py:296
  3.0 0.0 copy-start.1
  3.0 14.8 %all-to-all-start = ((bf16[64,2,6272]{2,1,0:T(2,128)(2,1)}), bf16[64,2,6272]{2,1,0:T(2,128)(2,1)S(1)}, u32[]{:S(2)}, u32[]{:S(2)}) async-start(bf16[64,2,6272]{2,1,0:T(2,128)(2,1)} %shard_map.59), calls=%async_computation | async-start | bytes 3211264 | tf_op jit(solution)/shard_map/all_to_all | solution.py:291
  17.8 0.0 copy-done.1
  17.8 32.0 %all-gather = bf16[2304,216]{1,0:T(8,128)(2,1)S(1)} all-gather(bf16[192,216]{1,0:T(8,128)(2,1)S(1)} %bitcast.14), channel_id=2, replica_groups=mesh['dp'=12,'x'=4,'y'=8,'core'=2] {'dp'}, dimensions={0}, use_global_device_ids=true | all-gather | bytes 1078272 | tf_op jit(solution)/shard_map/all_gather | solution.py:311
  49.8 0.9 shard_map.60.tall_ref
  50.7 7.6 %all-to-all-done.arrived_ref = bf16[64,2,6272]{2,1,0:T(2,128)(2,1)S(1)} async-done(((bf16[64,2,6272]{2,1,0:T(2,128)(2,1)}), bf16[64,2,6272]{2,1,0:T(2,128)(2,1)S(1)}, u32[]{:S(2)}, u32[]{:S(2)}) %all-to-all-start) | async-done | bytes 1605664 | tf_op jit(solution)/shard_map/all_to_all | solution.py:291
  58.3 0.3 shard_map.62
  58.6 2.9 %collective-permute-start = (bf16[64,1536]{1,0:T(8,128)(2,1)S(1)}, bf16[64,1536]{1,0:T(8,128)(2,1)S(1)}, u32[]{:S(2)}, u32[]{:S(2)}) collective-permute-start(bf16[64,1536]{1,0:T(8,128)(2,1)S(1)} %shard_map.62), channel_id=1, source_target_pairs={{0,1},{1,2},{2,3},{3,4},{4,5},{5,6},{6,7},{7,8},{8,9},{9,10},{10,1... | collective-permute-start | bytes 589832 | tf_op jit(solution)/shard_map/ppermute | solution.py:315
  61.5 0.0 copy-start
  61.5 4.0 %shard_map.61 = (bf16[512,4608]{1,0:T(8,128)(2,1)S(1)}, f32[512,384]{1,0:T(8,128)S(1)}, bf16[1536,384]{1,0:T(8,128)(2,1)S(1)}) custom-call(bf16[64,2,6272]{2,1,0:T(2,128)(2,1)S(1)} %all-to-all-done.arrived_ref, bf16[2592,192]{1,0:T(8,128)(2,1)S(1)} %shard_map.60.tall_ref), custom_call_target="tpu_custom_call" | custom-call | flops 1811939328 | tf_op jit(solution)/shard_map/pallas_call | solution.py:316
  65.5 0.0 collective-permute-done.rim_ref
  65.5 0.0 copy-done
  65.5 5.5 %shard_map.63 = (bf16[4,16,3072]{2,1,0:T(8,128)(2,1)}, f32[32,64,128]{2,1,0:T(8,128)S(1)}, f32[32,64,128]{2,1,0:T(8,128)S(1)}) custom-call(s32[1]{0:T(128)} %bitcast.core_ref, bf16[512,4608]{1,0:T(8,128)(2,1)S(1)} %get-tuple-element.12.columns_ref, f32[512,384]{1,0:T(8,128)S(1)} %get-tuple-element.13.linear_ref, ...), custom_call_target="tpu_custom_call" | custom-call | tf_op jit(solution)/shard_map/pallas_call | solution.py:330
  71.0 1.9 %collective-permute-start.1 = (f32[32,64,128]{2,1,0:T(8,128)S(1)}, f32[32,64,128]{2,1,0:T(8,128)S(1)}, u32[]{:S(2)}, u32[]{:S(2)}) collective-permute-start(f32[32,64,128]{2,1,0:T(8,128)S(1)} %get-tuple-element.17), channel_id=1, source_target_pairs={{0,1},{1,0},{2,3},{3,2},{4,5},{5,4},{6,7},{7,6},{8,9},{9,8},{10,11... | collective-permute-start | bytes 3145736 | tf_op jit(solution)/shard_map/ppermute | solution.py:346
  72.9 2.6 %collective-permute-done.1 = f32[32,64,128]{2,1,0:T(8,128)S(1)} collective-permute-done((f32[32,64,128]{2,1,0:T(8,128)S(1)}, f32[32,64,128]{2,1,0:T(8,128)S(1)}, u32[]{:S(2)}, u32[]{:S(2)}) %collective-permute-start.1) | collective-permute-done | bytes 1048608 | tf_op jit(solution)/shard_map/ppermute | solution.py:346
  75.5 0.2 add_convert_fusion
  75.7 22.4 %all_to_all.20.terms_ref = bf16[32,64,128]{2,1,0:T(8,128)(2,1)S(1)} all-to-all(bf16[32,64,128]{2,1,0:T(8,128)(2,1)S(1)} %add_convert_fusion), channel_id=1, replica_groups=mesh['dp'=12,'x'=4,'y'=8,'core'=2] {'x','y'}, dimensions={0} | all-to-all | bytes 1048576 | tf_op jit(solution)/shard_map/all_to_all | solution.py:291
  98.1 0.1 shard_map.64
  98.3 19.2 %all_to_all.21.sums_ref = f32[12,1,768]{2,1,0:T(1,128)S(1)} all-to-all(f32[12,1,768]{2,1,0:T(1,128)S(1)} %shard_map.64), channel_id=1, replica_groups=mesh['dp'=12,'x'=4,'y'=8,'core'=2] {'dp'}, dimensions={0} | all-to-all | bytes 73728 | tf_op jit(solution)/shard_map/all_to_all | solution.py:291
  117.5 21.6 %all_to_all.22.pieces_ref = f32[64,1,768]{2,1,0:T(1,128)S(1)} all-to-all(f32[64,1,768]{2,1,0:T(1,128)S(1)} %shard_map.65), channel_id=1, replica_groups=mesh['dp'=12,'x'=4,'y'=8,'core'=2] {'x','y','core'}, dimensions={0} | all-to-all | bytes 393216 | tf_op jit(solution)/shard_map/all_to_all | solution.py:291
  139.1 0.9 shard_map.66
  (1 shorter events, 0.0 us)
Async XLA Ops:
  3.0 14.8 %copy-start.1 = (bf16[216,192]{0,1:T(8,128)(2,1)S(1)}, bf16[216,192]{0,1:T(8,128)(2,1)}, u32[]{:S(2)}) copy-start(bf16[216,192]{0,1:T(8,128)(2,1)} %param.6) | copy-start | bytes 248836
  3.0 55.3 %all-to-all-start = ((bf16[64,2,6272]{2,1,0:T(2,128)(2,1)}), bf16[64,2,6272]{2,1,0:T(2,128)(2,1)S(1)}, u32[]{:S(2)}, u32[]{:S(2)}) async-start(bf16[64,2,6272]{2,1,0:T(2,128)(2,1)} %shard_map.59), calls=%async_computation | async-start | bytes 3211264 | tf_op jit(solution)/shard_map/all_to_all | solution.py:291
  58.6 6.9 %collective-permute-start = (bf16[64,1536]{1,0:T(8,128)(2,1)S(1)}, bf16[64,1536]{1,0:T(8,128)(2,1)S(1)}, u32[]{:S(2)}, u32[]{:S(2)}) collective-permute-start(bf16[64,1536]{1,0:T(8,128)(2,1)S(1)} %shard_map.62), channel_id=1, source_target_pairs={{0,1},{1,2},{2,3},{3,4},{4,5},{5,6},{6,7},{7,8},{8,9},{9,10},{10,1... | collective-permute-start | bytes 589832 | tf_op jit(solution)/shard_map/ppermute | solution.py:315
  61.5 4.0 %copy-start = (bf16[1,4,16,3072]{3,2,1,0:T(8,128)(2,1)S(1)}, bf16[1,4,16,3072]{3,2,1,0:T(8,128)(2,1)}, u32[]{:S(2)}) copy-start(bf16[1,4,16,3072]{3,2,1,0:T(8,128)(2,1)} %param.7) | copy-start | bytes 1179652
  71.0 4.5 %collective-permute-start.1 = (f32[32,64,128]{2,1,0:T(8,128)S(1)}, f32[32,64,128]{2,1,0:T(8,128)S(1)}, u32[]{:S(2)}, u32[]{:S(2)}) collective-permute-start(f32[32,64,128]{2,1,0:T(8,128)S(1)} %get-tuple-element.17), channel_id=1, source_target_pairs={{0,1},{1,0},{2,3},{3,2},{4,5},{5,4},{6,7},{7,6},{8,9},{9,8},{10,11... | collective-permute-start | bytes 3145736 | tf_op jit(solution)/shard_map/ppermute | solution.py:346

commit v6 on v5

--- a/solution.py
+++ b/solution.py
@@ -132,24 +132,22 @@
 
     for sx in range(2):
         for sy in range(2):
-            pick = [picker(sx, sy, sz) for sz in range(2)]
+            pick = jnp.concatenate([picker(sx, sy, sz) for sz in range(2)], axis=0)
             for vx in [3] if sx else range(4):
                 for vy in [3] if sy else range(4):
                     at = (vx * 4 + vy) * LINE
                     source = arrived_ref[:, :, at : at + LINE].reshape(NPOS, LINE)
-                    line = jnp.dot(pick[0], source, preferred_element_type=F32)
-                    before = jnp.dot(pick[1], source[:, 256:], preferred_element_type=F32)
-                    store_line(
-                        columns_ref, line.astype(BF16), before.astype(BF16),
-                        vx - 4 * sx, vy - 4 * sy, TAPS,
-                    )
+                    line = jnp.dot(pick[:NPOS], source[:, :256], preferred_element_type=F32)
+                    ends = jnp.dot(pick, source[:, 256:], preferred_element_type=F32).astype(BF16)
+                    line = jnp.concatenate([line.astype(BF16), ends[:NPOS]], axis=1)
+                    store_line(columns_ref, line, ends[NPOS:], vx - 4 * sx, vy - 4 * sy, TAPS)
     linear_ref[...] = jnp.dot(columns_ref[...], wide[...], preferred_element_type=F32)
 
 
 def layer_kernel(
     core_ref, columns_ref, linear_ref, first_ref, rim_ref, cotangent_ref,
-    activation_ref, kept_ref, given_ref,
-    front, linear, upstream, result, slopes, packed, left, turned_left,
+    active_ref, kept_ref, given_ref,
+    front, linear, upstream, slopes, packed, left, turned_left,
 ):
     rz, rx, ry = brick_rows((NPOS, 64), 0)
     m = lax.broadcasted_iota(jnp.int32, (NPOS, 64), 1)
@@ -182,25 +180,19 @@
                 row = (i * 2 + j) * NPOS + z * 16
                 value = linear[row : row + 16, :]
                 sigma = 1.0 / (1.0 + jnp.exp(-value))
-                active = value * sigma
+                active_ref[row : row + 16, :] = (value * sigma).astype(BF16)
                 slope = sigma * (1.0 + value * (1.0 - sigma))
                 incoming = []
                 for tile in range(3):
-                    lanes = slice(tile * 128, (tile + 1) * 128)
-                    parts = []
-                    for x in range(2):
-                        at = (x * 2 + i, z * 3 + tile, pl.ds(j, 8, stride=2), slice(None))
-                        parts.append(upstream[at])
-                        result[at] = active[x * 8 : x * 8 + 8, lanes]
+                    parts = [
+                        upstream[x * 2 + i, z * 3 + tile, pl.ds(j, 8, stride=2), :]
+                        for x in range(2)
+                    ]
                     incoming.append(jnp.concatenate(parts, axis=0))
                 incoming = jnp.concatenate(incoming, axis=1)
                 change = (incoming * slope).astype(BF16)
                 slopes[0, row : row + 16, :] = change[:, 0:C_OUT]
                 slopes[1, row : row + 16, :] = change[:, C_OUT:]
-    for tile in range(24):
-        for x in range(4):
-            activation_ref[x, :, tile * 128 : (tile + 1) * 128] = result[x, tile].astype(BF16)
-
     left[:, 64:128] = jnp.zeros((N_DP * 8, 64), F32)
     turned_left[:, N_DP * 8 :] = jnp.zeros((NPOS, NPOS - N_DP * 8), F32)
     for tap in range(TAPS):
@@ -242,6 +234,22 @@
             target[chip, rows + 1 :, :] = jnp.zeros((TERM - rows - 1, 128), F32)
 
 
+def finish_kernel(active_ref, activation_ref, result):
+    for i in range(2):
+        for j in range(2):
+            for z in range(8):
+                row = (i * 2 + j) * NPOS + z * 16
+                active = active_ref[row : row + 16, :].astype(F32)
+                for tile in range(3):
+                    for x in range(2):
+                        result[x * 2 + i, z * 3 + tile, pl.ds(j, 8, stride=2), :] = active[
+                            x * 8 : x * 8 + 8, tile * 128 : (tile + 1) * 128
+                        ]
+    for tile in range(24):
+        for x in range(4):
+            activation_ref[x, :, tile * 128 : (tile + 1) * 128] = result[x, tile].astype(BF16)
+
+
 def chip_sum_kernel(terms_ref, sums_ref):
     total = terms_ref[0].astype(F32)
     for source in range(1, N_CHIP):
@@ -327,13 +335,12 @@
     )(arrived, tall)
     core = lax.axis_index("core").astype(jnp.int32).reshape(1)
     term = shape((N_CHIP, TERM, 128), F32)
-    activation, kept, given = call(
+    active, kept, given = call(
         layer_kernel,
-        (shape((4, 16, 8 * LINE), BF16), term, term),
+        (shape((4 * NPOS, LINE), BF16), term, term),
         [
             pltpu.VMEM((2 * NPOS, 3 * DEPTH), BF16),
             pltpu.VMEM((4 * NPOS, LINE), F32),
-            pltpu.VMEM((4, 24, 16, 128), F32),
             pltpu.VMEM((4, 24, 16, 128), F32),
             pltpu.VMEM((2, 4 * NPOS, C_OUT), BF16),
             pltpu.VMEM((TERM * N_BRICK, 128), F32),
@@ -344,6 +351,13 @@
         megabytes=16,
     )(core, columns, linear, first, rim, cotangent.reshape(4, 16, 8 * LINE))
     taken = lax.ppermute(given, "core", [(0, 1), (1, 0)])
+    activation = call(
+        finish_kernel,
+        shape((4, 16, 8 * LINE), BF16),
+        [pltpu.VMEM((4, 24, 16, 128), F32)],
+        flops=1024 * 1024,
+    )(active)
+    taken, activation = lax.optimization_barrier((taken, activation))
     terms = spread((kept + taken).astype(BF16), ("x", "y"))
     sums = call(chip_sum_kernel, shape((N_DP, 1, WIDTH), F32))(terms)
     copies = call(scene_sum_kernel, shape((N_BRICK, 1, WIDTH), F32))(spread(sums, "dp"))

time: 140 us -> 140 us (level)
    pallas_call x1 -> x2, Pallas kernels: 5.45 us -> 5.49 us  [the longest x1 4.63 us: body(): call(layer_kernel, (shape((4 * NPOS, LINE), BF16), term, term), [pltpu.VM...]
where the time goes in v6:
time: 140 us; the launch traced here: 139 us
  blocking collectives  95.3 us (68%)
  starting transfers between devices  19.6 us (14%)
  Pallas kernels  14.1 us (10%)
  waiting for transfers between devices  9.37 us (7%)
    all_to_all x3, blocking collectives, spread(): return lax.all_to_all(block, axis, split_axis=0, concat_axis=0, tiled=True)  63.3 us
    all_gather x1, blocking collectives, body(): full_weight = lax.all_gather(weight.T, 'dp', axis=0, tiled=False)  32 us
    all_to_all x1, starting transfers between devices, spread(): return lax.all_to_all(block, axis, split_axis=0, concat_axis=0, tiled=True)  14.8 us
    all_to_all x1, waiting for transfers between devices, spread(): return lax.all_to_all(block, axis, split_axis=0, concat_axis=0, tiled=True)  7.61 us
    pallas_call x1, Pallas kernels, body(): call(layer_kernel, (shape((4 * NPOS, LINE), BF16), term, term), [pltpu.VM...  4.63 us
    pallas_call x1, Pallas kernels, body(): call(place_kernel, (shape((4 * NPOS, TAPS * DEPTH), BF16), shape((4 * NPO...  3.98 us
    ppermute x1, starting transfers between devices, body(): rim = lax.ppermute(rim, BRICK, [(i, i + 1) for i in range(N_BRICK - 1)])  2.87 us
  transfers between devices with their start and end apart: 3, of which 2 were waited for; matrix products, arithmetic and copies ran while one was open for 0% of the time, Pallas kernels for 4%

profile of v6, /device:TPU:1, one launch (start us, length us, event | category | flops | bytes accessed | tf_op | source)
XLA Modules:
  0.0 139.2 jit_solution(9268361782445954478)
XLA Ops:
  0.6 2.4 %shard_map.59 = bf16[64,2,6272]{2,1,0:T(2,128)(2,1)} custom-call(bf16[64,2,6144]{2,1,0:T(2,128)(2,1)} %bitcast.12, s32[2,64]{1,0:T(2,128)} %bitcast.16), custom_call_target="tpu_custom_call" | custom-call | tf_op jit(solution)/shard_map/pallas_call | solution.py:304
  3.0 0.0 copy-start.1
  3.0 14.8 %all-to-all-start = ((bf16[64,2,6272]{2,1,0:T(2,128)(2,1)}), bf16[64,2,6272]{2,1,0:T(2,128)(2,1)S(1)}, u32[]{:S(2)}, u32[]{:S(2)}) async-start(bf16[64,2,6272]{2,1,0:T(2,128)(2,1)} %shard_map.59), calls=%async_computation | async-start | bytes 3211264 | tf_op jit(solution)/shard_map/all_to_all | solution.py:299
  17.8 0.0 copy-done.1
  17.8 32.0 %all-gather = bf16[2304,216]{1,0:T(8,128)(2,1)S(1)} all-gather(bf16[192,216]{1,0:T(8,128)(2,1)S(1)} %bitcast.15), channel_id=2, replica_groups=mesh['dp'=12,'x'=4,'y'=8,'core'=2] {'dp'}, dimensions={0}, use_global_device_ids=true | all-gather | bytes 1078272 | tf_op jit(solution)/shard_map/all_gather | solution.py:319
  49.8 0.9 shard_map.60.tall_ref
  50.7 7.6 %all-to-all-done.arrived_ref = bf16[64,2,6272]{2,1,0:T(2,128)(2,1)S(1)} async-done(((bf16[64,2,6272]{2,1,0:T(2,128)(2,1)}), bf16[64,2,6272]{2,1,0:T(2,128)(2,1)S(1)}, u32[]{:S(2)}, u32[]{:S(2)}) %all-to-all-start) | async-done | bytes 1605664 | tf_op jit(solution)/shard_map/all_to_all | solution.py:299
  58.3 0.3 shard_map.62
  58.6 2.9 %collective-permute-start = (bf16[64,1536]{1,0:T(8,128)(2,1)S(1)}, bf16[64,1536]{1,0:T(8,128)(2,1)S(1)}, u32[]{:S(2)}, u32[]{:S(2)}) collective-permute-start(bf16[64,1536]{1,0:T(8,128)(2,1)S(1)} %shard_map.62), channel_id=1, source_target_pairs={{0,1},{1,2},{2,3},{3,4},{4,5},{5,6},{6,7},{7,8},{8,9},{9,10},{10,1... | collective-permute-start | bytes 589832 | tf_op jit(solution)/shard_map/ppermute | solution.py:323
  61.5 0.0 copy-start
  61.5 4.0 %shard_map.61 = (bf16[512,4608]{1,0:T(8,128)(2,1)S(1)}, f32[512,384]{1,0:T(8,128)S(1)}, bf16[1536,384]{1,0:T(8,128)(2,1)S(1)}) custom-call(bf16[64,2,6272]{2,1,0:T(2,128)(2,1)S(1)} %all-to-all-done.arrived_ref, bf16[2592,192]{1,0:T(8,128)(2,1)S(1)} %shard_map.60.tall_ref), custom_call_target="tpu_custom_call" | custom-call | flops 1811939328 | tf_op jit(solution)/shard_map/pallas_call | solution.py:324
  65.5 0.0 collective-permute-done.rim_ref
  65.5 0.0 copy-done
  65.5 4.6 %shard_map.63 = (bf16[512,384]{1,0:T(8,128)(2,1)S(1)}, f32[32,64,128]{2,1,0:T(8,128)S(1)}, f32[32,64,128]{2,1,0:T(8,128)S(1)}) custom-call(s32[1]{0:T(128)} %bitcast.core_ref, bf16[512,4608]{1,0:T(8,128)(2,1)S(1)} %get-tuple-element.14.columns_ref, f32[512,384]{1,0:T(8,128)S(1)} %get-tuple-element.15.linear_ref, ...), custom_call_target="tpu_custom_call" | custom-call | tf_op jit(solution)/shard_map/pallas_call | solution.py:338
  70.1 1.9 %collective-permute-start.1 = (f32[32,64,128]{2,1,0:T(8,128)S(1)}, f32[32,64,128]{2,1,0:T(8,128)S(1)}, u32[]{:S(2)}, u32[]{:S(2)}) collective-permute-start(f32[32,64,128]{2,1,0:T(8,128)S(1)} %get-tuple-element.17), channel_id=1, source_target_pairs={{0,1},{1,0},{2,3},{3,2},{4,5},{5,4},{6,7},{7,6},{8,9},{9,8},{10,11... | collective-permute-start | bytes 3145736 | tf_op jit(solution)/shard_map/ppermute | solution.py:353
  72.1 0.9 shard_map.64
  72.9 1.8 %collective-permute-done.1 = f32[32,64,128]{2,1,0:T(8,128)S(1)} collective-permute-done((f32[32,64,128]{2,1,0:T(8,128)S(1)}, f32[32,64,128]{2,1,0:T(8,128)S(1)}, u32[]{:S(2)}, u32[]{:S(2)}) %collective-permute-start.1) | collective-permute-done | bytes 1048608 | tf_op jit(solution)/shard_map/ppermute | solution.py:353
  74.7 0.2 add_convert_fusion
  74.9 22.5 %all_to_all.20.terms_ref = bf16[32,64,128]{2,1,0:T(8,128)(2,1)S(1)} all-to-all(bf16[32,64,128]{2,1,0:T(8,128)(2,1)S(1)} %add_convert_fusion), channel_id=1, replica_groups=mesh['dp'=12,'x'=4,'y'=8,'core'=2] {'x','y'}, dimensions={0} | all-to-all | bytes 1048576 | tf_op jit(solution)/shard_map/all_to_all | solution.py:299
  97.3 0.1 shard_map.65
  97.5 19.2 %all_to_all.21.sums_ref = f32[12,1,768]{2,1,0:T(1,128)S(1)} all-to-all(f32[12,1,768]{2,1,0:T(1,128)S(1)} %shard_map.65), channel_id=1, replica_groups=mesh['dp'=12,'x'=4,'y'=8,'core'=2] {'dp'}, dimensions={0} | all-to-all | bytes 73728 | tf_op jit(solution)/shard_map/all_to_all | solution.py:299
  116.7 21.6 %all_to_all.22.pieces_ref = f32[64,1,768]{2,1,0:T(1,128)S(1)} all-to-all(f32[64,1,768]{2,1,0:T(1,128)S(1)} %shard_map.66), channel_id=1, replica_groups=mesh['dp'=12,'x'=4,'y'=8,'core'=2] {'x','y','core'}, dimensions={0} | all-to-all | bytes 393216 | tf_op jit(solution)/shard_map/all_to_all | solution.py:299
  138.3 0.9 shard_map.67
  (1 shorter events, 0.0 us)
Async XLA Ops:
  3.0 14.8 %copy-start.1 = (bf16[216,192]{0,1:T(8,128)(2,1)S(1)}, bf16[216,192]{0,1:T(8,128)(2,1)}, u32[]{:S(2)}) copy-start(bf16[216,192]{0,1:T(8,128)(2,1)} %param.6) | copy-start | bytes 248836
  3.0 55.3 %all-to-all-start = ((bf16[64,2,6272]{2,1,0:T(2,128)(2,1)}), bf16[64,2,6272]{2,1,0:T(2,128)(2,1)S(1)}, u32[]{:S(2)}, u32[]{:S(2)}) async-start(bf16[64,2,6272]{2,1,0:T(2,128)(2,1)} %shard_map.59), calls=%async_computation | async-start | bytes 3211264 | tf_op jit(solution)/shard_map/all_to_all | solution.py:299
  58.6 6.9 %collective-permute-start = (bf16[64,1536]{1,0:T(8,128)(2,1)S(1)}, bf16[64,1536]{1,0:T(8,128)(2,1)S(1)}, u32[]{:S(2)}, u32[]{:S(2)}) collective-permute-start(bf16[64,1536]{1,0:T(8,128)(2,1)S(1)} %shard_map.62), channel_id=1, source_target_pairs={{0,1},{1,2},{2,3},{3,4},{4,5},{5,6},{6,7},{7,8},{8,9},{9,10},{10,1... | collective-permute-start | bytes 589832 | tf_op jit(solution)/shard_map/ppermute | solution.py:323
  61.5 4.0 %copy-start = (bf16[1,4,16,3072]{3,2,1,0:T(8,128)(2,1)S(1)}, bf16[1,4,16,3072]{3,2,1,0:T(8,128)(2,1)}, u32[]{:S(2)}) copy-start(bf16[1,4,16,3072]{3,2,1,0:T(8,128)(2,1)} %param.7) | copy-start | bytes 1179652
  70.1 4.6 %collective-permute-start.1 = (f32[32,64,128]{2,1,0:T(8,128)S(1)}, f32[32,64,128]{2,1,0:T(8,128)S(1)}, u32[]{:S(2)}, u32[]{:S(2)}) collective-permute-start(f32[32,64,128]{2,1,0:T(8,128)S(1)} %get-tuple-element.17), channel_id=1, source_target_pairs={{0,1},{1,0},{2,3},{3,2},{4,5},{5,4},{6,7},{7,6},{8,9},{9,8},{10,11... | collective-permute-start | bytes 3145736 | tf_op jit(solution)/shard_map/ppermute | solution.py:353

commit v7 on v6

--- a/solution.py
+++ b/solution.py
@@ -256,30 +256,34 @@
         total += terms_ref[source].astype(F32)
     last = N_DP * PIECE
     for d in range(N_DP):
-        for row in range(PIECE):
-            at = d * PIECE + row
-            sums_ref[d, :, row * 128 : (row + 1) * 128] = total[at : at + 1]
-        sums_ref[d, :, PIECE * 128 :] = jnp.concatenate(
-            [total[last : last + 1, d * 8 : d * 8 + 8], jnp.zeros((1, 120), F32)], axis=1
-        )
+        ends = total[last : last + 1, d * 8 : d * 8 + 8]
+        ends = jnp.concatenate([ends, jnp.zeros((1, 120), F32)], axis=1)
+        for core in range(2):
+            for row in range(PIECE):
+                at = d * PIECE + row
+                sums_ref[2 * d + core, :, row * 128 : (row + 1) * 128] = total[at : at + 1]
+            sums_ref[2 * d + core, :, PIECE * 128 :] = ends
 
 
 def scene_sum_kernel(sums_ref, copies_ref):
-    total = sums_ref[0]
-    for source in range(1, N_DP):
-        total += sums_ref[source]
-    for target in range(N_BRICK):
-        copies_ref[target] = total
+    for core in range(2):
+        total = sums_ref[core]
+        for source in range(1, N_DP):
+            total += sums_ref[2 * source + core]
+        for target in range(N_CHIP):
+            copies_ref[target, :, core * WIDTH : (core + 1) * WIDTH] = total
 
 
 def unpack_kernel(pieces_ref, grad_ref, packed):
-    for row in range(PIECE):
-        packed[row * N_BRICK : (row + 1) * N_BRICK, :] = pieces_ref[
-            :, 0, row * 128 : (row + 1) * 128
-        ]
+    for core in range(2):
+        for row in range(PIECE + 1):
+            at = core * WIDTH + row * 128
+            packed[pl.ds(row * N_BRICK + core, N_CHIP, stride=2), :] = pieces_ref[
+                :, 0, at : at + 128
+            ]
     grad_ref[0:128, :] = packed[0:SHARD, :].T
     grad_ref[128:C_OUT, 0:KEEP] = packed[SHARD : SHARD + KEEP, 0:64].T
-    grad_ref[128:C_OUT, KEEP:SPLIT] = pieces_ref[:, 0, PIECE * 128 : PIECE * 128 + 128][:, 0:8]
+    grad_ref[128:C_OUT, KEEP:SPLIT] = packed[ROWS : ROWS + N_BRICK, 0:8]
     grad_ref[128:C_OUT, SPLIT:SHARD] = packed[SHARD : SHARD + KEEP, 64:128].T
 
 
@@ -359,11 +363,14 @@
     )(active)
     taken, activation = lax.optimization_barrier((taken, activation))
     terms = spread((kept + taken).astype(BF16), ("x", "y"))
-    sums = call(chip_sum_kernel, shape((N_DP, 1, WIDTH), F32))(terms)
-    copies = call(scene_sum_kernel, shape((N_BRICK, 1, WIDTH), F32))(spread(sums, "dp"))
-    grad = call(unpack_kernel, shape((C_OUT, SHARD), F32), [pltpu.VMEM((ROWS, 128), F32)])(
-        spread(copies, BRICK)
-    )
+    sums = call(chip_sum_kernel, shape((2 * N_DP, 1, WIDTH), F32))(terms)
+    sums = spread(sums, ("dp", "core"))
+    copies = call(scene_sum_kernel, shape((N_CHIP, 1, 2 * WIDTH), F32))(sums)
+    grad = call(
+        unpack_kernel,
+        shape((C_OUT, SHARD), F32),
+        [pltpu.VMEM((ROWS + N_BRICK, 128), F32)],
+    )(spread(copies, ("x", "y")))
     return activation.reshape(cotangent.shape), grad.T
 
 

time: 140 us -> 139 us (level)
  blocking collectives: 95.3 us -> 93.2 us
    all_to_all x3, blocking collectives: 63.3 us -> 61.2 us  [spread(): return lax.all_to_all(block, axis, split_axis=0, concat_axis=0, tiled=True)]
where the time goes in v7:
time: 139 us; the launch traced here: 137 us
  blocking collectives  93.2 us (67%)
  starting transfers between devices  19.6 us (14%)
  Pallas kernels  14.1 us (10%)
  waiting for transfers between devices  9.37 us (7%)
    all_to_all x3, blocking collectives, spread(): return lax.all_to_all(block, axis, split_axis=0, concat_axis=0, tiled=True)  61.2 us
    all_gather x1, blocking collectives, body(): full_weight = lax.all_gather(weight.T, 'dp', axis=0, tiled=False)  32 us
    all_to_all x1, starting transfers between devices, spread(): return lax.all_to_all(block, axis, split_axis=0, concat_axis=0, tiled=True)  14.8 us
    all_to_all x1, waiting for transfers between devices, spread(): return lax.all_to_all(block, axis, split_axis=0, concat_axis=0, tiled=True)  7.61 us
    pallas_call x1, Pallas kernels, body(): call(layer_kernel, (shape((4 * NPOS, LINE), BF16), term, term), [pltpu.VM...  4.63 us
    pallas_call x1, Pallas kernels, body(): call(place_kernel, (shape((4 * NPOS, TAPS * DEPTH), BF16), shape((4 * NPO...  3.98 us
    ppermute x1, starting transfers between devices, body(): rim = lax.ppermute(rim, BRICK, [(i, i + 1) for i in range(N_BRICK - 1)])  2.87 us
  transfers between devices with their start and end apart: 3, of which 2 were waited for; matrix products, arithmetic and copies ran while one was open for 0% of the time, Pallas kernels for 4%

profile of v7, /device:TPU:1, one launch (start us, length us, event | category | flops | bytes accessed | tf_op | source)
XLA Modules:
  0.0 137.2 jit_solution(106733335426116240)
XLA Ops:
  0.6 2.4 %shard_map.59 = bf16[64,2,6272]{2,1,0:T(2,128)(2,1)} custom-call(bf16[64,2,6144]{2,1,0:T(2,128)(2,1)} %bitcast.12, s32[2,64]{1,0:T(2,128)} %bitcast.16), custom_call_target="tpu_custom_call" | custom-call | tf_op jit(solution)/shard_map/pallas_call | solution.py:308
  3.0 0.0 copy-start.1
  3.0 14.8 %all-to-all-start = ((bf16[64,2,6272]{2,1,0:T(2,128)(2,1)}), bf16[64,2,6272]{2,1,0:T(2,128)(2,1)S(1)}, u32[]{:S(2)}, u32[]{:S(2)}) async-start(bf16[64,2,6272]{2,1,0:T(2,128)(2,1)} %shard_map.59), calls=%async_computation | async-start | bytes 3211264 | tf_op jit(solution)/shard_map/all_to_all | solution.py:303
  17.8 0.0 copy-done.1
  17.8 32.0 %all-gather = bf16[2304,216]{1,0:T(8,128)(2,1)S(1)} all-gather(bf16[192,216]{1,0:T(8,128)(2,1)S(1)} %bitcast.15), channel_id=2, replica_groups=mesh['dp'=12,'x'=4,'y'=8,'core'=2] {'dp'}, dimensions={0}, use_global_device_ids=true | all-gather | bytes 1078272 | tf_op jit(solution)/shard_map/all_gather | solution.py:323
  49.8 0.9 shard_map.60.tall_ref
  50.7 7.6 %all-to-all-done.arrived_ref = bf16[64,2,6272]{2,1,0:T(2,128)(2,1)S(1)} async-done(((bf16[64,2,6272]{2,1,0:T(2,128)(2,1)}), bf16[64,2,6272]{2,1,0:T(2,128)(2,1)S(1)}, u32[]{:S(2)}, u32[]{:S(2)}) %all-to-all-start) | async-done | bytes 1605664 | tf_op jit(solution)/shard_map/all_to_all | solution.py:303
  58.3 0.3 shard_map.62
  58.6 2.9 %collective-permute-start = (bf16[64,1536]{1,0:T(8,128)(2,1)S(1)}, bf16[64,1536]{1,0:T(8,128)(2,1)S(1)}, u32[]{:S(2)}, u32[]{:S(2)}) collective-permute-start(bf16[64,1536]{1,0:T(8,128)(2,1)S(1)} %shard_map.62), channel_id=1, source_target_pairs={{0,1},{1,2},{2,3},{3,4},{4,5},{5,6},{6,7},{7,8},{8,9},{9,10},{10,1... | collective-permute-start | bytes 589832 | tf_op jit(solution)/shard_map/ppermute | solution.py:327
  61.5 0.0 copy-start
  61.5 4.0 %shard_map.61 = (bf16[512,4608]{1,0:T(8,128)(2,1)S(1)}, f32[512,384]{1,0:T(8,128)S(1)}, bf16[1536,384]{1,0:T(8,128)(2,1)S(1)}) custom-call(bf16[64,2,6272]{2,1,0:T(2,128)(2,1)S(1)} %all-to-all-done.arrived_ref, bf16[2592,192]{1,0:T(8,128)(2,1)S(1)} %shard_map.60.tall_ref), custom_call_target="tpu_custom_call" | custom-call | flops 1811939328 | tf_op jit(solution)/shard_map/pallas_call | solution.py:328
  65.5 0.0 collective-permute-done.rim_ref
  65.5 0.0 copy-done
  65.5 4.6 %shard_map.63 = (bf16[512,384]{1,0:T(8,128)(2,1)S(1)}, f32[32,64,128]{2,1,0:T(8,128)S(1)}, f32[32,64,128]{2,1,0:T(8,128)S(1)}) custom-call(s32[1]{0:T(128)} %bitcast.core_ref, bf16[512,4608]{1,0:T(8,128)(2,1)S(1)} %get-tuple-element.14.columns_ref, f32[512,384]{1,0:T(8,128)S(1)} %get-tuple-element.15.linear_ref, ...), custom_call_target="tpu_custom_call" | custom-call | tf_op jit(solution)/shard_map/pallas_call | solution.py:342
  70.1 1.9 %collective-permute-start.1 = (f32[32,64,128]{2,1,0:T(8,128)S(1)}, f32[32,64,128]{2,1,0:T(8,128)S(1)}, u32[]{:S(2)}, u32[]{:S(2)}) collective-permute-start(f32[32,64,128]{2,1,0:T(8,128)S(1)} %get-tuple-element.17), channel_id=1, source_target_pairs={{0,1},{1,0},{2,3},{3,2},{4,5},{5,4},{6,7},{7,6},{8,9},{9,8},{10,11... | collective-permute-start | bytes 3145736 | tf_op jit(solution)/shard_map/ppermute | solution.py:357
  72.1 0.9 shard_map.64
  72.9 1.8 %collective-permute-done.1 = f32[32,64,128]{2,1,0:T(8,128)S(1)} collective-permute-done((f32[32,64,128]{2,1,0:T(8,128)S(1)}, f32[32,64,128]{2,1,0:T(8,128)S(1)}, u32[]{:S(2)}, u32[]{:S(2)}) %collective-permute-start.1) | collective-permute-done | bytes 1048608 | tf_op jit(solution)/shard_map/ppermute | solution.py:357
  74.7 0.2 add_convert_fusion
  74.9 22.5 %all_to_all.20.terms_ref = bf16[32,64,128]{2,1,0:T(8,128)(2,1)S(1)} all-to-all(bf16[32,64,128]{2,1,0:T(8,128)(2,1)S(1)} %add_convert_fusion), channel_id=1, replica_groups=mesh['dp'=12,'x'=4,'y'=8,'core'=2] {'x','y'}, dimensions={0} | all-to-all | bytes 1048576 | tf_op jit(solution)/shard_map/all_to_all | solution.py:303
  97.3 0.1 shard_map.65
  97.5 24.1 %all_to_all.21.sums_ref = f32[24,1,768]{2,1,0:T(1,128)S(1)} all-to-all(f32[24,1,768]{2,1,0:T(1,128)S(1)} %shard_map.65), channel_id=1, replica_groups=mesh['dp'=12,'x'=4,'y'=8,'core'=2] {'dp','core'}, dimensions={0} | all-to-all | bytes 147456 | tf_op jit(solution)/shard_map/all_to_all | solution.py:303
  121.6 14.7 %all_to_all.22.pieces_ref = f32[32,1,1536]{2,1,0:T(1,128)S(1)} all-to-all(f32[32,1,1536]{2,1,0:T(1,128)S(1)} %shard_map.66), channel_id=1, replica_groups=mesh['dp'=12,'x'=4,'y'=8,'core'=2] {'x','y'}, dimensions={0} | all-to-all | bytes 393216 | tf_op jit(solution)/shard_map/all_to_all | solution.py:303
  136.2 0.9 shard_map.67
  (1 shorter events, 0.0 us)
Async XLA Ops:
  3.0 14.8 %copy-start.1 = (bf16[216,192]{0,1:T(8,128)(2,1)S(1)}, bf16[216,192]{0,1:T(8,128)(2,1)}, u32[]{:S(2)}) copy-start(bf16[216,192]{0,1:T(8,128)(2,1)} %param.6) | copy-start | bytes 248836
  3.0 55.3 %all-to-all-start = ((bf16[64,2,6272]{2,1,0:T(2,128)(2,1)}), bf16[64,2,6272]{2,1,0:T(2,128)(2,1)S(1)}, u32[]{:S(2)}, u32[]{:S(2)}) async-start(bf16[64,2,6272]{2,1,0:T(2,128)(2,1)} %shard_map.59), calls=%async_computation | async-start | bytes 3211264 | tf_op jit(solution)/shard_map/all_to_all | solution.py:303
  58.6 6.9 %collective-permute-start = (bf16[64,1536]{1,0:T(8,128)(2,1)S(1)}, bf16[64,1536]{1,0:T(8,128)(2,1)S(1)}, u32[]{:S(2)}, u32[]{:S(2)}) collective-permute-start(bf16[64,1536]{1,0:T(8,128)(2,1)S(1)} %shard_map.62), channel_id=1, source_target_pairs={{0,1},{1,2},{2,3},{3,4},{4,5},{5,6},{6,7},{7,8},{8,9},{9,10},{10,1... | collective-permute-start | bytes 589832 | tf_op jit(solution)/shard_map/ppermute | solution.py:327
  61.5 4.0 %copy-start = (bf16[1,4,16,3072]{3,2,1,0:T(8,128)(2,1)S(1)}, bf16[1,4,16,3072]{3,2,1,0:T(8,128)(2,1)}, u32[]{:S(2)}) copy-start(bf16[1,4,16,3072]{3,2,1,0:T(8,128)(2,1)} %param.7) | copy-start | bytes 1179652
  70.1 4.6 %collective-permute-start.1 = (f32[32,64,128]{2,1,0:T(8,128)S(1)}, f32[32,64,128]{2,1,0:T(8,128)S(1)}, u32[]{:S(2)}, u32[]{:S(2)}) collective-permute-start(f32[32,64,128]{2,1,0:T(8,128)S(1)} %get-tuple-element.17), channel_id=1, source_target_pairs={{0,1},{1,0},{2,3},{3,2},{4,5},{5,4},{6,7},{7,6},{8,9},{9,8},{10,11... | collective-permute-start | bytes 3145736 | tf_op jit(solution)/shard_map/ppermute | solution.py:357

commit v8 on v6

--- a/solution.py
+++ b/solution.py
@@ -20,7 +20,7 @@
 KEEP = 104
 PIECE = 5
 TERM = 64
-CHUNKS = 8
+CHUNKS = 4
 WIDTH = (PIECE + 1) * 128
 ROWS = N_BRICK * PIECE
 BRICK = ("x", "y", "core")

time: 140 us -> 139 us (level)
  no operation moved by 1% of the time
where the time goes in v8:
time: 139 us
  blocking collectives  95.3 us (69%)
  starting transfers between devices  19.6 us (14%)
  Pallas kernels  14 us (10%)
  waiting for transfers between devices  9.37 us (7%)
    all_to_all x3, blocking collectives, spread(): return lax.all_to_all(block, axis, split_axis=0, concat_axis=0, tiled=True)  63.3 us
    all_gather x1, blocking collectives, body(): full_weight = lax.all_gather(weight.T, 'dp', axis=0, tiled=False)  32 us
    all_to_all x1, starting transfers between devices, spread(): return lax.all_to_all(block, axis, split_axis=0, concat_axis=0, tiled=True)  14.8 us
    all_to_all x1, waiting for transfers between devices, spread(): return lax.all_to_all(block, axis, split_axis=0, concat_axis=0, tiled=True)  7.61 us
    pallas_call x1, Pallas kernels, body(): call(layer_kernel, (shape((4 * NPOS, LINE), BF16), term, term), [pltpu.VM...  4.63 us
    pallas_call x1, Pallas kernels, body(): call(place_kernel, (shape((4 * NPOS, TAPS * DEPTH), BF16), shape((4 * NPO...  3.99 us
    ppermute x1, starting transfers between devices, body(): rim = lax.ppermute(rim, BRICK, [(i, i + 1) for i in range(N_BRICK - 1)])  2.87 us
  transfers between devices with their start and end apart: 3, of which 2 were waited for; matrix products, arithmetic and copies ran while one was open for 0% of the time, Pallas kernels for 4%

profile of v8, /device:TPU:1, one launch (start us, length us, event | category | flops | bytes accessed | tf_op | source)
XLA Modules:
  0.0 139.1 jit_solution(524130474833981032)
XLA Ops:
  0.6 2.3 %shard_map.59 = bf16[64,2,6272]{2,1,0:T(2,128)(2,1)} custom-call(bf16[64,2,6144]{2,1,0:T(2,128)(2,1)} %bitcast.12, s32[2,64]{1,0:T(2,128)} %bitcast.16), custom_call_target="tpu_custom_call" | custom-call | tf_op jit(solution)/shard_map/pallas_call | solution.py:304
  2.9 0.0 copy-start.1
  2.9 14.8 %all-to-all-start = ((bf16[64,2,6272]{2,1,0:T(2,128)(2,1)}), bf16[64,2,6272]{2,1,0:T(2,128)(2,1)S(1)}, u32[]{:S(2)}, u32[]{:S(2)}) async-start(bf16[64,2,6272]{2,1,0:T(2,128)(2,1)} %shard_map.59), calls=%async_computation | async-start | bytes 3211264 | tf_op jit(solution)/shard_map/all_to_all | solution.py:299
  17.7 0.0 copy-done.1
  17.7 32.0 %all-gather = bf16[2304,216]{1,0:T(8,128)(2,1)S(1)} all-gather(bf16[192,216]{1,0:T(8,128)(2,1)S(1)} %bitcast.15), channel_id=2, replica_groups=mesh['dp'=12,'x'=4,'y'=8,'core'=2] {'dp'}, dimensions={0}, use_global_device_ids=true | all-gather | bytes 1078272 | tf_op jit(solution)/shard_map/all_gather | solution.py:319
  49.7 0.9 shard_map.60.tall_ref
  50.6 7.6 %all-to-all-done.arrived_ref = bf16[64,2,6272]{2,1,0:T(2,128)(2,1)S(1)} async-done(((bf16[64,2,6272]{2,1,0:T(2,128)(2,1)}), bf16[64,2,6272]{2,1,0:T(2,128)(2,1)S(1)}, u32[]{:S(2)}, u32[]{:S(2)}) %all-to-all-start) | async-done | bytes 1605664 | tf_op jit(solution)/shard_map/all_to_all | solution.py:299
  58.2 0.3 shard_map.62
  58.5 2.9 %collective-permute-start = (bf16[64,1536]{1,0:T(8,128)(2,1)S(1)}, bf16[64,1536]{1,0:T(8,128)(2,1)S(1)}, u32[]{:S(2)}, u32[]{:S(2)}) collective-permute-start(bf16[64,1536]{1,0:T(8,128)(2,1)S(1)} %shard_map.62), channel_id=1, source_target_pairs={{0,1},{1,2},{2,3},{3,4},{4,5},{5,6},{6,7},{7,8},{8,9},{9,10},{10,1... | collective-permute-start | bytes 589832 | tf_op jit(solution)/shard_map/ppermute | solution.py:323
  61.4 0.0 copy-start
  61.4 4.0 %shard_map.61 = (bf16[512,4608]{1,0:T(8,128)(2,1)S(1)}, f32[512,384]{1,0:T(8,128)S(1)}, bf16[1536,384]{1,0:T(8,128)(2,1)S(1)}) custom-call(bf16[64,2,6272]{2,1,0:T(2,128)(2,1)S(1)} %all-to-all-done.arrived_ref, bf16[2592,192]{1,0:T(8,128)(2,1)S(1)} %shard_map.60.tall_ref), custom_call_target="tpu_custom_call" | custom-call | flops 1811939328 | tf_op jit(solution)/shard_map/pallas_call | solution.py:324
  65.4 0.0 collective-permute-done.rim_ref
  65.4 0.0 copy-done
  65.4 4.6 %shard_map.63 = (bf16[512,384]{1,0:T(8,128)(2,1)S(1)}, f32[32,64,128]{2,1,0:T(8,128)S(1)}, f32[32,64,128]{2,1,0:T(8,128)S(1)}) custom-call(s32[1]{0:T(128)} %bitcast.core_ref, bf16[512,4608]{1,0:T(8,128)(2,1)S(1)} %get-tuple-element.14.columns_ref, f32[512,384]{1,0:T(8,128)S(1)} %get-tuple-element.15.linear_ref, ...), custom_call_target="tpu_custom_call" | custom-call | tf_op jit(solution)/shard_map/pallas_call | solution.py:338
  70.0 1.9 %collective-permute-start.1 = (f32[32,64,128]{2,1,0:T(8,128)S(1)}, f32[32,64,128]{2,1,0:T(8,128)S(1)}, u32[]{:S(2)}, u32[]{:S(2)}) collective-permute-start(f32[32,64,128]{2,1,0:T(8,128)S(1)} %get-tuple-element.17), channel_id=1, source_target_pairs={{0,1},{1,0},{2,3},{3,2},{4,5},{5,4},{6,7},{7,6},{8,9},{9,8},{10,11... | collective-permute-start | bytes 3145736 | tf_op jit(solution)/shard_map/ppermute | solution.py:353
  72.0 0.9 shard_map.64
  72.8 1.8 %collective-permute-done.1 = f32[32,64,128]{2,1,0:T(8,128)S(1)} collective-permute-done((f32[32,64,128]{2,1,0:T(8,128)S(1)}, f32[32,64,128]{2,1,0:T(8,128)S(1)}, u32[]{:S(2)}, u32[]{:S(2)}) %collective-permute-start.1) | collective-permute-done | bytes 1048608 | tf_op jit(solution)/shard_map/ppermute | solution.py:353
  74.6 0.2 add_convert_fusion
  74.8 22.5 %all_to_all.20.terms_ref = bf16[32,64,128]{2,1,0:T(8,128)(2,1)S(1)} all-to-all(bf16[32,64,128]{2,1,0:T(8,128)(2,1)S(1)} %add_convert_fusion), channel_id=1, replica_groups=mesh['dp'=12,'x'=4,'y'=8,'core'=2] {'x','y'}, dimensions={0} | all-to-all | bytes 1048576 | tf_op jit(solution)/shard_map/all_to_all | solution.py:299
  97.2 0.1 shard_map.65
  97.4 19.2 %all_to_all.21.sums_ref = f32[12,1,768]{2,1,0:T(1,128)S(1)} all-to-all(f32[12,1,768]{2,1,0:T(1,128)S(1)} %shard_map.65), channel_id=1, replica_groups=mesh['dp'=12,'x'=4,'y'=8,'core'=2] {'dp'}, dimensions={0} | all-to-all | bytes 73728 | tf_op jit(solution)/shard_map/all_to_all | solution.py:299
  116.6 21.6 %all_to_all.22.pieces_ref = f32[64,1,768]{2,1,0:T(1,128)S(1)} all-to-all(f32[64,1,768]{2,1,0:T(1,128)S(1)} %shard_map.66), channel_id=1, replica_groups=mesh['dp'=12,'x'=4,'y'=8,'core'=2] {'x','y','core'}, dimensions={0} | all-to-all | bytes 393216 | tf_op jit(solution)/shard_map/all_to_all | solution.py:299
  138.2 0.9 shard_map.67
  (1 shorter events, 0.0 us)
Async XLA Ops:
  2.9 14.8 %copy-start.1 = (bf16[216,192]{0,1:T(8,128)(2,1)S(1)}, bf16[216,192]{0,1:T(8,128)(2,1)}, u32[]{:S(2)}) copy-start(bf16[216,192]{0,1:T(8,128)(2,1)} %param.6) | copy-start | bytes 248836
  2.9 55.3 %all-to-all-start = ((bf16[64,2,6272]{2,1,0:T(2,128)(2,1)}), bf16[64,2,6272]{2,1,0:T(2,128)(2,1)S(1)}, u32[]{:S(2)}, u32[]{:S(2)}) async-start(bf16[64,2,6272]{2,1,0:T(2,128)(2,1)} %shard_map.59), calls=%async_computation | async-start | bytes 3211264 | tf_op jit(solution)/shard_map/all_to_all | solution.py:299
  58.5 6.9 %collective-permute-start = (bf16[64,1536]{1,0:T(8,128)(2,1)S(1)}, bf16[64,1536]{1,0:T(8,128)(2,1)S(1)}, u32[]{:S(2)}, u32[]{:S(2)}) collective-permute-start(bf16[64,1536]{1,0:T(8,128)(2,1)S(1)} %shard_map.62), channel_id=1, source_target_pairs={{0,1},{1,2},{2,3},{3,4},{4,5},{5,6},{6,7},{7,8},{8,9},{9,10},{10,1... | collective-permute-start | bytes 589832 | tf_op jit(solution)/shard_map/ppermute | solution.py:323
  61.4 4.0 %copy-start = (bf16[1,4,16,3072]{3,2,1,0:T(8,128)(2,1)S(1)}, bf16[1,4,16,3072]{3,2,1,0:T(8,128)(2,1)}, u32[]{:S(2)}) copy-start(bf16[1,4,16,3072]{3,2,1,0:T(8,128)(2,1)} %param.7) | copy-start | bytes 1179652
  70.0 4.6 %collective-permute-start.1 = (f32[32,64,128]{2,1,0:T(8,128)S(1)}, f32[32,64,128]{2,1,0:T(8,128)S(1)}, u32[]{:S(2)}, u32[]{:S(2)}) collective-permute-start(f32[32,64,128]{2,1,0:T(8,128)S(1)} %get-tuple-element.17), channel_id=1, source_target_pairs={{0,1},{1,0},{2,3},{3,2},{4,5},{5,4},{6,7},{7,6},{8,9},{9,8},{10,11... | collective-permute-start | bytes 3145736 | tf_op jit(solution)/shard_map/ppermute | solution.py:353
